TPU v7x, 256 devices: a whole 4x4x8 slice. The times are simulated.
256 devices in a mesh: basin: 128 (over x, y, z), rep: 2 (over core).
Axes of the slice: x: 4, y: 4, z: 8, core: 2. Of those that a mesh axis runs over, the one named last changes fastest.
Arguments:
- forcing: bfloat16 [16, 32, 65536], P(None, None, ('basin', 'rep')), may hold values from -6 to 6
- w_in: bfloat16 [1024, 32], replicated, may hold values from -1 to 1
- w_rec: bfloat16 [1024, 256], replicated, may hold values from -0.375 to 0.375
- bias: float32 [1024], replicated, may hold values from -3 to 3
- w_out: float32 [256], replicated, may hold values from -0.375 to 0.375
- uh_shape: float32 [65536], P(('basin', 'rep')), may hold values from 1.5 to 4
- uh_scale: float32 [65536], P(('basin', 'rep')), may hold values from 0.5 to 4
- reach_tier: int32 [65536], P(('basin', 'rep')), may hold values from 0 to 3, as said below
- reach_dest: int32 [65536], P(('basin', 'rep')), may hold values from -1 to 65535, as said below
- out_cot: float32 [16, 65536], P(None, ('basin', 'rep')), may hold values from -0.0625 to 0.0625
Outputs:
- outflow: float32 [16, 65536], P(None, ('basin', 'rep'))
- grad_w_in: float32 [1024, 32], replicated
- grad_w_rec: float32 [1024, 256], replicated
- grad_bias: float32 [1024], replicated
- grad_w_out: float32 [256], replicated
Inputs may be any that keep to these rules, and one draw needn't show every extreme that they name: `reach_tier`: every device holds reaches of every tier. `reach_dest`: -1 for a reach that leaves the network (all reaches of tier 4 - 1 among them); else the global index of a reach of the next tier on a device with the same rep index and a basin index from the own to the own + 2; of one device's reaches of one tier, at most 8 drain into reaches of one device, and on every device 8 reaches of tier 0 drain into its own reaches.
All inputs are finite; a program needn't handle non-finite values.
Results may differ from a plain program's by a relative error of at most 0.0034.
Values sent between devices are 32-bit elements; how exact they have to be, the bound alone decides.
A program may use at most 128 MiB of HBM per device.

v0:
```python
import jax
import jax.numpy as jnp
from jax import lax
from jax.sharding import PartitionSpec as P

UHLEN = 8
LEVELS = 4
CAP = 8
SPREAD = 3


def from_behind(block, axis, distance):
    devices = range(lax.axis_size(axis))
    route = [(i - distance, i) for i in devices if i - distance in devices]
    return lax.ppermute(block, axis, route)


def hydro_kernel(uh_shape, uh_scale, length):
    lag_days = (jnp.arange(length, dtype=jnp.float32) + 1.0)[:, None]
    weights = jnp.exp((uh_shape[None, :] - 1.0) * jnp.log(lag_days) - lag_days / uh_scale[None, :])
    return weights / jnp.sum(weights, axis=0, keepdims=True)


def convolve(kernel, series):
    length = kernel.shape[0]
    day_count = series.shape[0]
    padded = jnp.concatenate([jnp.zeros((length - 1, series.shape[1]), jnp.float32), series], 0)
    summed = jnp.zeros_like(series)
    for lag_index in range(length):
        start = length - 1 - lag_index
        summed = summed + kernel[lag_index][None, :] * padded[start : start + day_count]
    return summed


def correlate(kernel, series):
    length = kernel.shape[0]
    day_count = series.shape[0]
    padded = jnp.concatenate([series, jnp.zeros((length - 1, series.shape[1]), jnp.float32)], 0)
    summed = jnp.zeros_like(series)
    for lag_index in range(length):
        summed = summed + kernel[lag_index][None, :] * padded[lag_index : lag_index + day_count]
    return summed


def lstm_forward(forcing, w_in, w_rec, bias, w_out):
    width = w_rec.shape[1]
    reaches = forcing.shape[2]

    def step(state_pair, forcing_now):
        state_h, state_c = state_pair
        h_low = state_h.astype(jnp.bfloat16)
        preact = jnp.dot(w_in, forcing_now, preferred_element_type=jnp.float32)
        preact = preact + jnp.dot(w_rec, h_low, preferred_element_type=jnp.float32) + bias[:, None]
        gate_i = jax.nn.sigmoid(preact[:width])
        gate_f = jax.nn.sigmoid(preact[width : 2 * width])
        gate_g = jnp.tanh(preact[2 * width : 3 * width])
        gate_o = jax.nn.sigmoid(preact[3 * width :])
        cell_now = gate_f * state_c + gate_i * gate_g
        hidden = gate_o * jnp.tanh(cell_now)
        readout = jnp.dot(w_out, hidden, precision=lax.Precision.HIGHEST)
        return (
            (hidden, cell_now),
            (
                jax.nn.softplus(readout),
                h_low,
                state_c,
                cell_now,
                gate_i,
                gate_f,
                gate_g,
                gate_o,
                readout,
            ),
        )

    zeros = jnp.zeros((width, reaches), jnp.float32)
    _, saved = lax.scan(step, (zeros, zeros), forcing)
    return saved


def lstm_backward(forcing, w_rec, w_out, saved, grad_runoff):
    width = w_rec.shape[1]
    reaches = forcing.shape[2]
    _, h_low, cell_prev, cell_all, gate_i, gate_f, gate_g, gate_o, readout = saved

    def step(state_pair, inputs_now):
        grad_h_next, grad_c_next, acc_in, acc_rec, acc_bias, acc_out = state_pair
        forcing_now, hl_now, cp_now, ce_now, gi_now, gf_now, gg_now, go_now, read_now, gq_now = (
            inputs_now
        )
        grad_read = jax.nn.sigmoid(read_now) * gq_now
        tanh_c = jnp.tanh(ce_now)
        hidden = go_now * tanh_c
        acc_out = acc_out + jnp.dot(hidden, grad_read, precision=lax.Precision.HIGHEST)
        grad_h = w_out[:, None] * grad_read[None, :] + grad_h_next
        grad_c = grad_h * go_now * (1.0 - tanh_c * tanh_c) + grad_c_next
        grad_z = jnp.concatenate(
            [
                grad_c * gg_now * gi_now * (1.0 - gi_now),
                grad_c * cp_now * gf_now * (1.0 - gf_now),
                grad_c * gi_now * (1.0 - gg_now * gg_now),
                grad_h * tanh_c * go_now * (1.0 - go_now),
            ],
            0,
        )
        grad_z_low = grad_z.astype(jnp.bfloat16)
        acc_in = acc_in + jnp.dot(grad_z_low, forcing_now.T, preferred_element_type=jnp.float32)
        acc_rec = acc_rec + jnp.dot(grad_z_low, hl_now.T, preferred_element_type=jnp.float32)
        acc_bias = acc_bias + jnp.sum(grad_z, axis=1)
        grad_h_prev = jnp.dot(w_rec.T, grad_z_low, preferred_element_type=jnp.float32)
        return ((grad_h_prev, grad_c * gf_now, acc_in, acc_rec, acc_bias, acc_out), None)

    zeros = jnp.zeros((width, reaches), jnp.float32)
    start_state = (
        zeros,
        zeros,
        jnp.zeros((4 * width, forcing.shape[1]), jnp.float32),
        jnp.zeros((4 * width, width), jnp.float32),
        jnp.zeros((4 * width,), jnp.float32),
        jnp.zeros((width,), jnp.float32),
    )
    inputs_all = (
        forcing,
        h_low,
        cell_prev,
        cell_all,
        gate_i,
        gate_f,
        gate_g,
        gate_o,
        readout,
        grad_runoff,
    )
    final_state, _ = lax.scan(step, start_state, inputs_all, reverse=True)
    return (final_state[2], final_state[3], final_state[4], final_state[5])


def per_device(
    forcing, w_in, w_rec, bias, w_out, uh_shape, uh_scale, reach_tier, reach_dest, out_cot
):
    reaches = forcing.shape[2]
    rep_count = lax.axis_size("rep")
    own_basin = lax.axis_index("basin")
    saved = lstm_forward(forcing, w_in, w_rec, bias, w_out)
    runoff = saved[0]
    kernel = hydro_kernel(uh_shape, uh_scale, UHLEN)
    linked = reach_dest >= 0
    dest_basin = jnp.where(linked, reach_dest // (reaches * rep_count), own_basin)
    dest_local = jnp.where(linked, reach_dest % reaches, 0)
    owners = SPREAD
    placed = dest_basin - own_basin
    key_ids = reach_tier * owners + placed
    onehot = (
        (key_ids[:, None] == jnp.arange(LEVELS * owners, dtype=jnp.int32)[None, :])
        & linked[:, None]
    ).astype(jnp.int32)
    slot_rank = jnp.sum((jnp.cumsum(onehot, axis=0) - onehot) * onehot, axis=1)
    column = placed * CAP + slot_rank
    slot_ids = jnp.arange(owners * CAP, dtype=jnp.int32)
    senders = []
    for tier_now in range(LEVELS - 1):
        chosen = (column[:, None] == slot_ids[None, :]) & (linked & (reach_tier == tier_now))[
            :, None
        ]
        senders.append(chosen.astype(jnp.float32))
    target_col = reach_tier * CAP + slot_rank
    matched = placed[:, None, None] == jnp.arange(owners, dtype=jnp.int32)[None, :, None]
    matched = matched & (
        target_col[:, None, None] == jnp.arange(LEVELS * CAP, dtype=jnp.int32)[None, None, :]
    )
    matched = matched & linked[:, None, None]
    targets = jnp.sum(jnp.where(matched, dest_local[:, None, None] + 1, 0), axis=0)
    rows_in = [targets[0]]
    for lag_index in range(1, SPREAD):
        rows_in.append(from_behind(targets[lag_index], "basin", lag_index))
    arrived = jnp.stack(rows_in, 0)
    receivers = []
    for tier_now in range(LEVELS - 1):
        slot_target = arrived[:, tier_now * CAP : (tier_now + 1) * CAP].reshape(-1)
        receivers.append(
            (slot_target[:, None] - 1 == jnp.arange(reaches, dtype=jnp.int32)[None, :]).astype(
                jnp.float32
            )
        )

    def send_up(returning):
        pieces = [returning[:, :CAP]]
        for lag_index in range(1, SPREAD):
            pieces.append(
                from_behind(
                    returning[:, lag_index * CAP : (lag_index + 1) * CAP], "basin", -lag_index
                )
            )
        return jnp.concatenate(pieces, 1)

    inflow = jnp.zeros_like(runoff)
    for tier_now in range(LEVELS - 1):
        flow_now = convolve(kernel, runoff + inflow)
        outgoing = jnp.dot(flow_now, senders[tier_now], precision=lax.Precision.HIGHEST)
        send_pieces = [outgoing[:, :CAP]]
        for send_lag_index in range(1, SPREAD):
            send_pieces.append(
                from_behind(
                    outgoing[:, send_lag_index * CAP : (send_lag_index + 1) * CAP],
                    "basin",
                    send_lag_index,
                )
            )
        incoming = jnp.concatenate(send_pieces, 1)
        inflow = inflow + jnp.dot(incoming, receivers[tier_now], precision=lax.Precision.HIGHEST)
    outflow = convolve(kernel, runoff + inflow)
    grad_out = out_cot
    for tier_now in range(LEVELS - 2, -1, -1):
        grad_in = correlate(kernel, grad_out)
        returning = jnp.dot(grad_in, receivers[tier_now].T, precision=lax.Precision.HIGHEST)
        coming_back = send_up(returning)
        grad_out = grad_out + jnp.dot(
            coming_back, senders[tier_now].T, precision=lax.Precision.HIGHEST
        )
    grad_runoff = correlate(kernel, grad_out)
    local_grads = lstm_backward(forcing, w_rec, w_out, saved, grad_runoff)
    grad_in_w, grad_rec_w, grad_bias_v, grad_out_w = lax.psum(
        (local_grads[0], local_grads[1], local_grads[2], local_grads[3]), ("basin", "rep")
    )
    return (outflow, grad_in_w, grad_rec_w, grad_bias_v, grad_out_w)


def solution(mesh):
    placed = (
        P(None, None, ("basin", "rep")),
        P(),
        P(),
        P(),
        P(),
        P(("basin", "rep")),
        P(("basin", "rep")),
        P(("basin", "rep")),
        P(("basin", "rep")),
        P(None, ("basin", "rep")),
    )
    return jax.shard_map(
        per_device,
        mesh=mesh,
        in_specs=placed,
        out_specs=(P(None, ("basin", "rep")), P(), P(), P(), P()),
        check_vma=False,
    )
```

profile of v0, /device:TPU:1, one launch (start us, length us, event | category | flops | bytes accessed | tf_op | source)
XLA Modules:
  0.0 541.1 jit_solution(15955801998748353090)
XLA Ops:
  12.7 80.5 %while.56 = (s32[]{:T(128)}, f32[256,256]{0,1:T(8,128)S(1)}, f32[256,256]{0,1:T(8,128)S(1)}, f32[16,256]{1,0:T(8,128)S(1)}, bf16[16,256,256]{1,2,0:T(8,128)(2,1)...) while((s32[]{:T(128)}, f32[256,256]{0,1:T(8,128)S(1)}, ...), condition=%wide.region_2.3_spmd.clone, body=%wide.region_1.2_spmd.clone.sunk | while | flops 153552384 | bytes 8619741 | solution.py:77
  93.6 4.4 collective-permute-start
  97.9 4.9 collective-permute-start.1
  103.0 4.8 collective-permute-start.2
  107.8 3.1 collective-permute-start.3
  115.4 4.0 collective-permute-start.4
  119.4 5.1 collective-permute-start.5
  128.3 4.9 collective-permute-start.6
  133.2 5.2 collective-permute-start.7
  141.8 2.5 collective-permute-done.12
  144.3 3.1 collective-permute-done.13
  148.4 110.0 %while.57 = (s32[]{:T(128)}, f32[256,256]{0,1:T(8,128)S(1)}, f32[256,256]{0,1:T(8,128)S(1)}, f32[1024,32]{0,1:T(8,128)S(1)}, f32[1024,256]{1,0:T(8,128)S(1)}, /*...) while((s32[]{:T(128)}, f32[256,256]{0,1:T(8,128)S(1)}, ...), condition=%wide.region_9.10_spmd.clone, body=%wide.region_7.9_spmd.clone.sunk | while | flops 291441152 | bytes 14330131 | solution.py:134
  151.3 1.4 convolution_add_fusion.11
  158.2 1.4 convolution_add_fusion.11
  165.1 1.4 convolution_add_fusion.11
  171.9 1.4 convolution_add_fusion.11
  178.8 1.4 convolution_add_fusion.11
  185.7 1.4 convolution_add_fusion.11
  192.6 1.4 convolution_add_fusion.11
  199.4 1.4 convolution_add_fusion.11
  206.3 1.4 convolution_add_fusion.11
  213.2 1.4 convolution_add_fusion.11
  220.1 1.4 convolution_add_fusion.11
  226.9 1.4 convolution_add_fusion.11
  233.8 1.4 convolution_add_fusion.11
  240.7 1.4 convolution_add_fusion.11
  247.6 1.4 convolution_add_fusion.11
  254.4 1.4 convolution_add_fusion.11
  259.5 92.3 %all-reduce.8 = (f32[1024]{0:T(1024)}, f32[256]{0:T(256)}) all-reduce(f32[1024]{0:T(1024)S(1)} %get-tuple-element.483, f32[256]{0:T(256)S(1)} %get-tuple-element.484), channel_id=1, replica_groups=mesh['basin'=128,'rep'=2] {'basin','rep'}, use_global_device_ids=true, to_apply=%region_12.13 | all-reduce | flops 1280 | bytes 10240 | tf_op jit(solution)/shard_map/psum | solution.py:222
  351.7 178.7 %all-reduce.12.cloned.1.call-done = (f32[1024,32]{0,1:T(8,128)}, f32[1024,256]{1,0:T(8,128)}) async-done(((f32[1024,32]{0,1:T(8,128)}, f32[1024,256]{1,0:T(8,128)}), (f32[1024,32]{0,1:T(8,128)}, f32[1024,256]{1,0:T(8,128)})) %all-reduce.12.cloned.1.call-update) | async-done | bytes 1179664 | tf_op jit(solution)/shard_map/psum | solution.py:222
  530.5 1.6 copy.94
  532.0 2.3 copy.95
  (460 shorter events, 185.0 us)
Async XLA Ops:
  7.2 523.3 %all-reduce.12.cloned.1.call-start = ((), (), s32[]{:S(2)}) async-start(), calls=%async_computation | async-start | bytes 2359296 | tf_op jit(solution)/shard_map/psum | solution.py:222
  12.6 80.6 %copy-start.4 = (s32[256]{0:T(256)S(1)}, s32[256]{0:T(256)}, u32[]{:S(2)}) copy-start(s32[256]{0:T(256)} %param.21) | copy-start | bytes 3076
  12.7 99.2 %copy-start.5 = (f32[16,256]{1,0:T(8,128)S(1)}, f32[16,256]{1,0:T(8,128)}, u32[]{:S(2)}) copy-start(f32[16,256]{1,0:T(8,128)} %param.23) | copy-start | bytes 49156
  12.7 4.6 copy-start.3
  17.7 4.6 copy-start.3
  22.8 4.6 copy-start.3
  27.8 4.6 copy-start.3
  32.8 4.6 copy-start.3
  42.8 4.5 copy-start.3
  47.8 4.6 copy-start.3
  52.9 4.6 copy-start.3
  57.9 4.5 copy-start.3
  62.9 4.6 copy-start.3
  67.9 4.6 copy-start.3
  73.0 4.6 copy-start.3
  78.0 4.6 copy-start.3
  83.0 4.6 copy-start.3
  88.1 4.6 copy-start.3
  93.6 21.3 %collective-permute-start = (f32[16,8]{1,0:T(8,128)S(1)}, f32[16,8]{1,0:T(8,128)S(1)}, u32[]{:S(2)}, u32[]{:S(2)}) collective-permute-start(f32[16,8]{1,0:T(8,128)S(1)} %get-tuple-element.770), channel_id=1, source_target_pairs={{0,2},{2,4},{4,6},{6,8},{8,10},{10,12},{12,14},{14,16},{16,18},{18... | collective-permute-start | bytes 1544 | tf_op jit(solution)/shard_map/ppermute | solution.py:15
  97.9 16.9 %collective-permute-start.1 = (f32[16,8]{1,0:T(8,128)S(1)}, f32[16,8]{1,0:T(8,128)S(1)}, u32[]{:S(2)}, u32[]{:S(2)}) collective-permute-start(f32[16,8]{1,0:T(8,128)S(1)} %get-tuple-element.769), channel_id=1, source_target_pairs={{0,4},{2,6},{4,8},{6,10},{8,12},{10,14},{12,16},{14,18},{16,20},{1... | collective-permute-start | bytes 1544 | tf_op jit(solution)/shard_map/ppermute | solution.py:15
  103.0 7.9 %collective-permute-start.2 = (s32[32]{0:T(128)S(1)}, s32[32]{0:T(128)S(1)}, u32[]{:S(2)}, u32[]{:S(2)}) collective-permute-start(s32[32]{0:T(128)S(1)} %get-tuple-element.784), channel_id=1, source_target_pairs={{0,2},{2,4},{4,6},{6,8},{8,10},{10,12},{12,14},{14,16},{16,18},{18... | collective-permute-start | bytes 392 | tf_op jit(solution)/shard_map/ppermute | solution.py:15
  107.8 3.8 collective-permute-start.3
  112.2 12.3 %collective-permute-start.8 = (f32[16,8]{1,0:T(8,128)S(1)}, f32[16,8]{1,0:T(8,128)S(1)}, u32[]{:S(2)}, u32[]{:S(2)}) collective-permute-start(f32[16,8]{1,0:T(8,128)S(1)} %get-tuple-element.761), channel_id=1, source_target_pairs={{2,0},{4,2},{6,4},{8,6},{10,8},{12,10},{14,12},{16,14},{18,16},{20... | collective-permute-start | bytes 1544 | tf_op jit(solution)/shard_map/ppermute | solution.py:15
  113.6 11.0 %collective-permute-start.9 = (f32[16,8]{1,0:T(8,128)S(1)}, f32[16,8]{1,0:T(8,128)S(1)}, u32[]{:S(2)}, u32[]{:S(2)}) collective-permute-start(f32[16,8]{1,0:T(8,128)S(1)} %get-tuple-element.760), channel_id=1, source_target_pairs={{4,0},{6,2},{8,4},{10,6},{12,8},{14,10},{16,12},{18,14},{20,16},{2... | collective-permute-start | bytes 1544 | tf_op jit(solution)/shard_map/ppermute | solution.py:15
  115.4 12.3 %collective-permute-start.4 = (f32[16,8]{1,0:T(8,128)S(1)}, f32[16,8]{1,0:T(8,128)S(1)}, u32[]{:S(2)}, u32[]{:S(2)}) collective-permute-start(f32[16,8]{1,0:T(8,128)S(1)} %get-tuple-element.767), channel_id=1, source_target_pairs={{0,2},{2,4},{4,6},{6,8},{8,10},{10,12},{12,14},{14,16},{16,18},{18... | collective-permute-start | bytes 1544 | tf_op jit(solution)/shard_map/ppermute | solution.py:15
  119.4 8.3 %collective-permute-start.5 = (f32[16,8]{1,0:T(8,128)S(1)}, f32[16,8]{1,0:T(8,128)S(1)}, u32[]{:S(2)}, u32[]{:S(2)}) collective-permute-start(f32[16,8]{1,0:T(8,128)S(1)} %get-tuple-element.766), channel_id=1, source_target_pairs={{0,4},{2,6},{4,8},{6,10},{8,12},{10,14},{12,16},{14,18},{16,20},{1... | collective-permute-start | bytes 1544 | tf_op jit(solution)/shard_map/ppermute | solution.py:15
  125.1 13.3 %collective-permute-start.10 = (f32[16,8]{1,0:T(8,128)S(1)}, f32[16,8]{1,0:T(8,128)S(1)}, u32[]{:S(2)}, u32[]{:S(2)}) collective-permute-start(f32[16,8]{1,0:T(8,128)S(1)} %get-tuple-element.758), channel_id=1, source_target_pairs={{2,0},{4,2},{6,4},{8,6},{10,8},{12,10},{14,12},{16,14},{18,16},{20... | collective-permute-start | bytes 1544 | tf_op jit(solution)/shard_map/ppermute | solution.py:15
  126.4 12.0 %collective-permute-start.11 = (f32[16,8]{1,0:T(8,128)S(1)}, f32[16,8]{1,0:T(8,128)S(1)}, u32[]{:S(2)}, u32[]{:S(2)}) collective-permute-start(f32[16,8]{1,0:T(8,128)S(1)} %get-tuple-element.757), channel_id=1, source_target_pairs={{4,0},{6,2},{8,4},{10,6},{12,8},{14,10},{16,12},{18,14},{20,16},{2... | collective-permute-start | bytes 1544 | tf_op jit(solution)/shard_map/ppermute | solution.py:15
  128.3 13.3 %collective-permute-start.6 = (f32[16,8]{1,0:T(8,128)S(1)}, f32[16,8]{1,0:T(8,128)S(1)}, u32[]{:S(2)}, u32[]{:S(2)}) collective-permute-start(f32[16,8]{1,0:T(8,128)S(1)} %get-tuple-element.764), channel_id=1, source_target_pairs={{0,2},{2,4},{4,6},{6,8},{8,10},{10,12},{12,14},{14,16},{16,18},{18... | collective-permute-start | bytes 1544 | tf_op jit(solution)/shard_map/ppermute | solution.py:15
  133.2 8.4 %collective-permute-start.7 = (f32[16,8]{1,0:T(8,128)S(1)}, f32[16,8]{1,0:T(8,128)S(1)}, u32[]{:S(2)}, u32[]{:S(2)}) collective-permute-start(f32[16,8]{1,0:T(8,128)S(1)} %get-tuple-element.763), channel_id=1, source_target_pairs={{0,4},{2,6},{4,8},{6,10},{8,12},{10,14},{12,16},{14,18},{16,20},{1... | collective-permute-start | bytes 1544 | tf_op jit(solution)/shard_map/ppermute | solution.py:15
  139.0 5.3 collective-permute-start.12
  140.3 7.1 %collective-permute-start.13 = (f32[16,8]{1,0:T(8,128)S(1)}, f32[16,8]{1,0:T(8,128)S(1)}, u32[]{:S(2)}, u32[]{:S(2)}) collective-permute-start(f32[16,8]{1,0:T(8,128)S(1)} %get-tuple-element.754), channel_id=1, source_target_pairs={{4,0},{6,2},{8,4},{10,6},{12,8},{14,10},{16,12},{18,14},{20,16},{2... | collective-permute-start | bytes 1544 | tf_op jit(solution)/shard_map/ppermute | solution.py:15
  (19 other events, 53.7 us)
Sparse Core Ops, SparseCore 0:
  259.6 270.8 all-reduce.11
where the time goes:
time: 547 us; the launch traced here: 541 us
  waiting for transfers between devices  185 us (34%)
  matrix products  110 us (20%)
  blocking collectives  92.3 us (17%)
  other arithmetic  85.1 us (16%)
  starting transfers between devices  44.1 us (8%)
  between operations  14.5 us (3%)
  local copies, waits for them, and re-layouts  7.36 us (1%)
    psum x1, waiting for transfers between devices, per_device(): lax.psum((local_grads[0], local_grads[1], local_grads[2], local_grads[3])...  179 us
    psum x1, blocking collectives, per_device(): lax.psum((local_grads[0], local_grads[1], local_grads[2], local_grads[3])...  92.3 us
    ppermute x14, starting transfers between devices, from_behind(): return lax.ppermute(block, axis, route)  44.1 us
    dynamic_update_slice x32, other arithmetic, lstm_forward(): _, saved = lax.scan(step, (zeros, zeros), forcing)  30 us
    dot_general x16, matrix products, step(): jnp.dot(grad_z_low, hl_now.T, preferred_element_type=jnp.float32)  22.2 us
    dot_general x16, matrix products, step(): jnp.dot(w_rec, h_low, preferred_element_type=jnp.float32)  22 us
    mul x16, other arithmetic, step(): grad_c * gg_now * gi_now * (1.0 - gi_now)  21.7 us
    mul x16, other arithmetic, step(): grad_c * gf_now  20.8 us
  transfers between devices with their start and end apart: 15, of which 4 were waited for; matrix products, arithmetic and copies ran while one was open for 1% of the time, Pallas kernels for 0%

commit v1 on v0

v1 whole, which is shorter than its diff:
```python
import jax
import jax.numpy as jnp
from jax import lax
from jax.experimental import pallas as pl
from jax.experimental.pallas import tpu as pltpu
from jax.sharding import PartitionSpec as P

MESH = pl.DeviceIdType.MESH
VMEM = pltpu.VMEM
f32 = jnp.float32
bf16 = jnp.bfloat16
DAYS = 16
HID = 256
FEAT = 32
REACH = 256
UHLEN = 8
XROWS = 304
GROWS = 1040
CHUNK = 32
SEMS = 200
NT = (((1,), (1,)), ((), ()))


class Place:
    def __init__(self):
        self.b = lax.axis_index("basin")
        self.r = lax.axis_index("rep")
        self.x = self.b // 32
        self.y = (self.b // 8) % 4
        self.z = self.b % 8
        self.q = self.x * 4 + self.y

    def core(self):
        return (self.b, 1 - self.r)

    def plane(self, d):
        px = lax.rem(self.x + d // 4, 4)
        py = lax.rem(self.y + d % 4, 4)
        return (px * 32 + py * 8 + self.z, self.r), px * 4 + py

    def plane_from(self, d):
        return lax.rem(self.x + 4 - d // 4, 4) * 4 + lax.rem(self.y + 4 - d % 4, 4)

    def line(self, d):
        pz = lax.rem(self.z + d, 8)
        return (self.x * 32 + self.y * 8 + pz, self.r), pz

    def line_from(self, d):
        return lax.rem(self.z + 8 - d, 8)

    def along(self, d):
        return (lax.rem(self.b + 128 + d, 128), self.r)


class Copies:
    def __init__(self, send, recv):
        self.send = send
        self.recv = recv
        self.all = []

    def __call__(self, src, dst, device):
        i = len(self.all)
        copy = pltpu.make_async_remote_copy(
            src_ref=src,
            dst_ref=dst,
            send_sem=self.send.at[i],
            recv_sem=self.recv.at[i],
            device_id=device,
            device_id_type=MESH,
        )
        copy.start()
        self.all.append(copy)
        return copy

    def drain(self):
        for copy in self.all:
            copy.wait_send()


def rows(start, size):
    return pl.ds(pl.multiple_of(start, 8), size)


def split3(v):
    hi = v.astype(bf16).astype(f32)
    mid = (v - hi).astype(bf16).astype(f32)
    return hi, mid, v - hi - mid


def hydro(shape_row, scale_row):
    lag = lax.broadcasted_iota(jnp.int32, (UHLEN, REACH), 0).astype(f32) + 1.0
    u = jnp.exp((shape_row - 1.0) * jnp.log(lag) - lag / scale_row)
    return u / jnp.sum(u, axis=0, keepdims=True)


def convolve(uh, series, pad):
    pad[8:24] = series
    total = uh[0:1] * series
    for m in range(1, UHLEN):
        total = total + uh[m : m + 1] * pad[8 - m : 24 - m]
    return total


def correlate(uh, series, pad):
    pad[8:24] = series
    total = uh[0:1] * series
    for m in range(1, UHLEN):
        total = total + uh[m : m + 1] * pad[8 + m : 24 + m]
    return total


def gather(blocks, index):
    halves = []
    for h in range(2):
        idx = jnp.broadcast_to(index[:, h * 128 : (h + 1) * 128], (DAYS, 128))
        lane = jnp.bitwise_and(idx, 127)
        block = jnp.right_shift(idx, 7)
        total = jnp.zeros((DAYS, 128), f32)
        for i in range(6):
            source = blocks[i // 2][:, (i % 2) * 128 : (i % 2 + 1) * 128]
            picked = jnp.take_along_axis(source, lane, axis=1)
            total = jnp.where(block == i, picked, total)
        halves.append(total)
    return jnp.concatenate(halves, 1)


def kernel(
    forcing, w_in_t, w_rec, bias, w_out, uh_shape, uh_scale, dest, cot,
    o_flow, o_in, o_rec, o_bias, o_out,
    W, WT, wcol, x, gates, cells, gz, gh, gcn, rd, grd,
    accA, accB, pad, adj, par, parb, route, fS, fR,
    bufA, rsA, zA, bufB, zB, xyB, outB, send, recv,
):
    p = Place()
    cp = Copies(send, recv)

    barrier = pltpu.get_barrier_semaphore()
    partners = [p.core()]
    partners += [p.plane(d)[0] for d in range(1, 16)]
    partners += [p.line(d)[0] for d in range(1, 8)]
    partners += [p.along(d) for d in (1, 2, 3, 4, 5, 6, -1, -2, -3, -4, -5, -6)]
    for device in partners:
        pl.semaphore_signal(barrier, inc=1, device_id=device, device_id_type=MESH)

    pad[...] = jnp.zeros_like(pad)
    uh = hydro(uh_shape[...], uh_scale[...])
    dest_row = dest[...]
    linked = dest_row >= 0
    ahead = jnp.right_shift(dest_row, 9) - p.b
    index = jnp.where(linked, ahead * REACH + jnp.bitwise_and(dest_row, REACH - 1), -1)
    row8 = lax.broadcasted_iota(jnp.int32, (8, REACH), 0)
    par[0] = jnp.where(
        row8 == 0, uh_shape[...], jnp.where(row8 == 1, uh_scale[...], index.astype(f32))
    )
    adj[0] = correlate(uh, cot[...], pad)

    for k in range(0, 1024, 128):
        half = 0.5 if k // 256 == 2 else 0.25
        back = 0.25 if k // 256 >= 2 else 0.125
        block = w_rec[k : k + 128].astype(f32)
        W[k : k + 128, 0:256] = (block * half).astype(bf16)
        WT[:, k : k + 128] = (block.T * back).astype(bf16)
        part = w_in_t[:, k : k + 128].astype(f32) * (2.0 * half)
        hi, mid, lo = split3(bias[:, k : k + 128] * (2.0 * half))
        row = lax.broadcasted_iota(jnp.int32, (96, 128), 0)
        rest = jnp.where(row == 0, hi, jnp.where(row == 1, mid, jnp.where(row == 2, lo, 0.0)))
        W[k : k + 128, 256:304] = jnp.concatenate([part, rest], 0).T[:, 0:48].astype(bf16)
    row16 = lax.broadcasted_iota(jnp.int32, (16, REACH), 0)
    hi, mid, lo = split3(w_out[...] * 0.5)
    W[1024:1040, 0:256] = jnp.where(
        row16 == 0, hi, jnp.where(row16 == 1, mid, jnp.where(row16 == 2, lo, 0.0))
    ).astype(bf16)
    W[1024:1040, 256:304] = jnp.zeros((16, 48), bf16)
    wcol[...] = jnp.broadcast_to(w_out[...], (128, HID)).T

    x[0, 0:256] = jnp.zeros((HID, REACH), bf16)
    ones = jnp.where(row16 < 3, 1.0, 0.0).astype(bf16)
    for t in range(DAYS):
        x[t, 256:288] = forcing[t]
        x[t, 288:304] = ones
    x[DAYS, 256:304] = jnp.zeros((48, REACH), bf16)
    cells[0] = jnp.zeros((HID, REACH), f32)

    def forward(t, _):
        pre = jnp.dot(W[...], x[t], preferred_element_type=f32)
        rd[pl.ds(t, 1)] = jnp.sum(pre[1024:1032], axis=0, keepdims=True)
        for c in range(0, HID, CHUNK):
            s = pl.ds(c, CHUNK)
            ti = jnp.tanh(pre[c : c + CHUNK])
            tf = jnp.tanh(pre[HID + c : HID + c + CHUNK])
            tg = jnp.tanh(pre[2 * HID + c : 2 * HID + c + CHUNK])
            to = jnp.tanh(pre[3 * HID + c : 3 * HID + c + CHUNK])
            cell = 0.5 * ((tf + 1.0) * cells[t, s] + (ti + 1.0) * tg)
            gates[0, t, s] = ti
            gates[1, t, s] = tf
            gates[2, t, s] = tg
            gates[3, t, s] = to
            cells[t + 1, s] = cell
            x[t + 1, s] = ((to + 1.0) * jnp.tanh(cell)).astype(bf16)
        return 0

    lax.fori_loop(0, 6, forward, 0)

    pl.semaphore_wait(barrier, len(partners))
    adj_in = [cp(adj.at[0], adj.at[d], p.along(-d)) for d in range(1, 7)]
    par_in = [cp(par.at[0], par.at[d], p.along(-d)) for d in range(1, 5)]
    parb_in = [cp(par.at[0], parb.at[d - 1], p.along(d)) for d in (1, 2)]

    lax.fori_loop(6, DAYS, forward, 0)
    last = jnp.dot(W[1024:1040], x[DAYS], preferred_element_type=f32)
    rd[DAYS : DAYS + 1] = jnp.sum(last, axis=0, keepdims=True)
    readout = rd[1 : DAYS + 1]

    runoff = jnp.maximum(readout, 0.0) + jnp.log1p(jnp.exp(-jnp.abs(readout)))
    fS[0] = convolve(uh, runoff, pad)

    def send_flow(n):
        return [cp(fS.at[n], fR.at[n, d - 1], p.along(d)) for d in (1, 2)]

    flow_in = send_flow(0)

    for copy in par_in + adj_in:
        copy.wait_recv()
    level = [adj[d] for d in range(7)]
    kernels = [uh] + [hydro(par[d, 0:1], par[d, 1:2]) for d in range(1, 5)]
    indices = [index] + [par[d, 2:3].astype(jnp.int32) for d in range(1, 5)]
    start = level
    for count in (5, 3, 1):
        level = [
            start[j] + correlate(kernels[j], gather(level[j : j + 3], indices[j]), pad)
            for j in range(count)
        ]
    grad_runoff = level[0]
    grad_read = (0.5 * jnp.tanh(0.5 * readout) + 0.5) * grad_runoff
    grd[0:8] = jnp.zeros((8, REACH), f32)
    grd[8:24] = grad_read

    for copy in parb_in:
        copy.wait_recv()
    target = lax.broadcasted_iota(jnp.int32, (REACH, REACH), 0)
    for j in range(3):
        source = index if j == 0 else parb[j - 1, 2:3].astype(jnp.int32)
        route[j] = jnp.where(target == source - j * REACH, 1.0, 0.0).astype(bf16)

    def inflow(n):
        total = jnp.zeros((DAYS, REACH), f32)
        for j in range(3):
            flow = fS[n] if j == 0 else fR[n, j - 1]
            parts = jnp.concatenate(split3(flow), 0).astype(bf16)
            moved = lax.dot_general(parts, route[j], NT, preferred_element_type=f32)
            total = total + moved[0:16] + moved[16:32] + moved[32:48]
        return total

    accA[...] = jnp.zeros_like(accA)
    accB[...] = jnp.zeros_like(accB)
    gh[...] = jnp.zeros_like(gh)
    gcn[...] = jnp.zeros_like(gcn)

    def elementwise(t):
        gr = grd[pl.ds(t + 8, 1)]
        for c in range(0, HID, CHUNK):
            s = pl.ds(c, CHUNK)
            w = jnp.concatenate([wcol[s], wcol[s]], 1)
            ti = gates[0, t, s]
            tf = gates[1, t, s]
            tg = gates[2, t, s]
            to = gates[3, t, s]
            tc = jnp.tanh(cells[t + 1, s])
            ghw = (w * gr + gh[s]) * (1.0 + to)
            gc = ghw * (1.0 - tc * tc) + gcn[s]
            gci = gc * (1.0 + ti)
            gcf = gc * (1.0 + tf)
            gz[c : c + CHUNK] = (gci * ((1.0 - ti) * tg)).astype(bf16)
            gz[HID + c : HID + c + CHUNK] = (gcf * ((1.0 - tf) * cells[t, s])).astype(bf16)
            gz[2 * HID + c : 2 * HID + c + CHUNK] = (gci * (1.0 - tg * tg)).astype(bf16)
            gz[3 * HID + c : 3 * HID + c + CHUNK] = (ghw * ((1.0 - to) * tc)).astype(bf16)
            gcn[s] = gcf * 0.5

    def read_rows(row):
        hi, mid, _ = split3(row)
        return jnp.where(row16 == 0, hi, jnp.where(row16 == 1, mid, 0.0)).astype(bf16)

    def inputs_grad(t):
        small = lax.dot_general(
            x[t, 256:304], gz[0:1024], NT, preferred_element_type=f32
        )
        for j in range(8):
            accB[0, j] += small[0:24, j * 128 : (j + 1) * 128]
            accB[1, j] += small[24:48, j * 128 : (j + 1) * 128]

    def backward(i, _):
        t = DAYS - 1 - i
        elementwise(t)
        gh[...] = jnp.dot(WT[...], gz[0:1024], preferred_element_type=f32)
        gz[1024:1040] = read_rows(grd[pl.ds(t + 7, 1)])
        accA[...] += lax.dot_general(gz[...], x[t, 0:256], NT, preferred_element_type=f32)
        inputs_grad(t)
        return 0

    lax.fori_loop(0, 5, backward, 0)
    for n in (0, 1):
        for copy in flow_in:
            copy.wait_recv()
        fS[n + 1] = convolve(uh, runoff + inflow(n), pad)
        flow_in = send_flow(n + 1)
        lax.fori_loop(5 + 5 * n, 10 + 5 * n, backward, 0)

    own = p.r * 512
    other = (1 - p.r) * 512
    core = p.core()
    core_in = [
        cp(accA.at[rows(other + c * 256, 256)], bufA.at[pl.ds(c * 256, 256)], core)
        for c in range(2)
    ]
    elementwise(0)
    inputs_grad(0)
    last = lax.dot_general(
        read_rows(grd[DAYS + 7 : DAYS + 8]), x[DAYS, 0:256], NT, preferred_element_type=f32
    )
    out_row = jnp.sum(last + accA[1024:1040], axis=0, keepdims=True)
    for j in range(2):
        accB[1, j, 11:12] = out_row[:, j * 128 : (j + 1) * 128]
    core_b = cp(accB.at[1 - p.r], bufB, core)

    plane_in = []
    for c in range(2):
        core_in[c].wait_recv()
        for k in range(0, 256, 64):
            accA[rows(own + c * 256 + k, 64)] += bufA[c * 256 + k : c * 256 + k + 64]
        batch = []
        for d in range(1, 16):
            device, q = p.plane(d)
            batch.append(cp(accA.at[rows(own + c * 256 + q * 16, 16)], rsA.at[c, d - 1], device))
        plane_in.append(batch)
    core_b.wait_recv()
    accB[p.r] += bufB[...]
    line_b = []
    for d in range(1, 8):
        device, z = p.line(d)
        line_b.append(cp(accB.at[p.r, z], zB.at[d - 1], device))

    for copy in flow_in:
        copy.wait_recv()
    o_flow[...] = convolve(uh, runoff + inflow(2), pad)

    line_in = []
    for c in range(2):
        total = accA[rows(own + c * 256 + p.q * 16, 16)]
        for d in range(1, 16):
            plane_in[c][d - 1].wait_recv()
            total = total + rsA[c, d - 1]
        zA[c, p.z] = total
        mine = zA.at[c, p.z]
        line_in.append([cp(mine, mine, p.line(d)[0]) for d in range(1, 8)])
    total = accB[p.r, p.z]
    for d in range(1, 8):
        line_b[d - 1].wait_recv()
        total = total + zB[d - 1]
    xyB[p.q] = total
    mine = xyB.at[p.q]
    plane_b = [cp(mine, mine, p.plane(d)[0]) for d in range(1, 16)]

    factor = jnp.where(p.r == 0, 0.0625, 0.125).astype(f32)
    gathered = []
    passed = []
    for c in range(2):
        for copy in line_in[c]:
            copy.wait_recv()
        total = zA[c, 0]
        for z in range(1, 8):
            total = total + zA[c, z]
        mine = o_rec.at[rows(own + c * 256 + p.q * 16, 16)]
        mine[...] = total * factor
        gathered.append([cp(mine, mine, p.plane(d)[0]) for d in range(1, 16)])
        passed.append(cp(mine, mine, core))
    for copy in plane_b:
        copy.wait_recv()
    total = xyB[0]
    for q in range(1, 16):
        total = total + xyB[q]
    outB[p.r, p.z] = total
    mine = outB.at[p.r, p.z]
    gathered_b = [cp(mine, mine, p.line(d)[0]) for d in range(1, 8)]
    passed.append(cp(mine, mine, core))
    for c in range(2):
        for d in range(1, 16):
            gathered[c][d - 1].wait_recv()
            piece = o_rec.at[rows(own + c * 256 + p.plane_from(d) * 16, 16)]
            passed.append(cp(piece, piece, core))
    for d in range(1, 8):
        gathered_b[d - 1].wait_recv()
        piece = outB.at[p.r, p.line_from(d)]
        passed.append(cp(piece, piece, core))
    for copy in passed:
        copy.wait_recv()

    for j in range(8):
        s = slice(j * 128, (j + 1) * 128)
        back = 0.25 if j >= 4 else 0.125
        o_in[0:24, s] = outB[0, j] * back
        o_in[24:32, s] = outB[1, j, 0:8] * back
        o_bias[:, s] = outB[1, j, 8:9] * back
        if j < 2:
            o_out[:, s] = outB[1, j, 11:12] * 0.5
    cp.drain()


def per_device(
    forcing, w_in, w_rec, bias, w_out, uh_shape, uh_scale, reach_tier, reach_dest, out_cot
):
    vmem = pl.BlockSpec(memory_space=VMEM)
    flow, g_in, g_rec, g_bias, g_out = pl.pallas_call(
        kernel,
        out_shape=[
            jax.ShapeDtypeStruct((DAYS, REACH), f32),
            jax.ShapeDtypeStruct((FEAT, 1024), f32),
            jax.ShapeDtypeStruct((1024, HID), f32),
            jax.ShapeDtypeStruct((1, 1024), f32),
            jax.ShapeDtypeStruct((1, HID), f32),
        ],
        in_specs=[vmem] * 9,
        out_specs=[vmem] * 5,
        scratch_shapes=[
            VMEM((GROWS, XROWS), bf16),
            VMEM((HID, 1024), bf16),
            VMEM((HID, 128), f32),
            VMEM((DAYS + 1, XROWS, REACH), bf16),
            VMEM((4, DAYS, HID, REACH), f32),
            VMEM((DAYS + 1, HID, REACH), f32),
            VMEM((GROWS, REACH), bf16),
            VMEM((HID, REACH), f32),
            VMEM((HID, REACH), f32),
            VMEM((24, REACH), f32),
            VMEM((24, REACH), f32),
            VMEM((GROWS, HID), f32),
            VMEM((2, 8, 24, 128), f32),
            VMEM((32, REACH), f32),
            VMEM((7, DAYS, REACH), f32),
            VMEM((5, 8, REACH), f32),
            VMEM((2, 8, REACH), f32),
            VMEM((3, REACH, REACH), bf16),
            VMEM((3, DAYS, REACH), f32),
            VMEM((3, 2, DAYS, REACH), f32),
            VMEM((512, HID), f32),
            VMEM((2, 15, 16, HID), f32),
            VMEM((2, 8, 16, HID), f32),
            VMEM((8, 24, 128), f32),
            VMEM((7, 24, 128), f32),
            VMEM((16, 24, 128), f32),
            VMEM((2, 8, 24, 128), f32),
            pltpu.SemaphoreType.DMA((SEMS,)),
            pltpu.SemaphoreType.DMA((SEMS,)),
        ],
        compiler_params=pltpu.CompilerParams(
            collective_id=0, has_side_effects=True, vmem_limit_bytes=50 * 2**20
        ),
        name="river",
    )(
        forcing,
        w_in.T,
        w_rec,
        bias.reshape(1, 1024),
        w_out.reshape(1, HID),
        uh_shape.reshape(1, REACH),
        uh_scale.reshape(1, REACH),
        reach_dest.reshape(1, REACH),
        out_cot,
    )
    return (flow, g_in.T, g_rec, g_bias.reshape(1024), g_out.reshape(HID))


def solution(mesh):
    placed = (
        P(None, None, ("basin", "rep")),
        P(),
        P(),
        P(),
        P(),
        P(("basin", "rep")),
        P(("basin", "rep")),
        P(("basin", "rep")),
        P(("basin", "rep")),
        P(None, ("basin", "rep")),
    )
    return jax.shard_map(
        per_device,
        mesh=mesh,
        in_specs=placed,
        out_specs=(P(None, ("basin", "rep")), P(), P(), P(), P()),
        check_vma=False,
    )
```

time: 547 us -> 72.2 us (0.13); the launches traced: 541 us -> 71.9 us
  waiting for transfers between devices: 185 us -> 0 us
  matrix products: 110 us -> 0 us
  blocking collectives: 92.3 us -> 0 us
  other arithmetic: 85.1 us -> 0 us
  Pallas kernels: 0 us -> 63.6 us
  starting transfers between devices: 44.1 us -> 0 us
  between operations: 14.5 us -> 0.69 us
    psum x1 -> x0, waiting for transfers between devices: 179 us -> none  [per_device(): lax.psum((local_grads[0], local_grads[1], local_grads[2], local_grads[3])...]
    dot_general x124 -> x0, matrix products: 110 us -> none  [the longest x16 22.2 us: step(): jnp.dot(grad_z_low, hl_now.T, preferred_element_type=jnp.float32)]
    psum x1 -> x0, blocking collectives: 92.3 us -> none  [per_device(): lax.psum((local_grads[0], local_grads[1], local_grads[2], local_grads[3])...]
    pallas_call x0 -> x1, Pallas kernels: none -> 63.6 us  [per_device(): pl.pallas_call(kernel, out_shape=[jax.ShapeDtypeStruct((DAYS, REACH), f32...]
    mul x64 -> x0, other arithmetic: 44.6 us -> none  [the longest x16 21.7 us: step(): grad_c * gg_now * gi_now * (1.0 - gi_now)]
    ppermute x14 -> x0, starting transfers between devices: 44.1 us -> none  [from_behind(): return lax.ppermute(block, axis, route)]
    dynamic_update_slice x32 -> x0, other arithmetic: 30 us -> none  [lstm_forward(): _, saved = lax.scan(step, (zeros, zeros), forcing)]
    ppermute x14 -> x0, waiting for transfers between devices: 6.29 us -> none  [from_behind(): return lax.ppermute(block, axis, route)]
  transfers between devices with their start and end apart: 15 -> 0, of which waited for: 4 -> 0; matrix products, arithmetic and copies ran while one was open for 1% -> 0% of each run, Pallas kernels for 0% -> 0%
where the time goes in v1:
time: 72.2 us; the launch traced here: 71.9 us
  Pallas kernels  63.6 us (88%)
  local copies, waits for them, and re-layouts  7.64 us (11%)
    pallas_call x1, Pallas kernels, per_device(): pl.pallas_call(kernel, out_shape=[jax.ShapeDtypeStruct((DAYS, REACH), f32...  63.6 us
    unnamed x23, local copies, waits for them, and re-layouts  7.64 us

profile of v1, /device:TPU:1, one launch (start us, length us, event | category | flops | bytes accessed | tf_op | source)
XLA Modules:
  0.0 71.9 jit_solution(11867307469482743418)
XLA Ops:
  0.6 0.0 copy-start.8
  0.6 0.0 copy-start.4
  0.7 0.0 copy-start.6
  0.7 0.0 copy-start.7
  0.7 0.0 copy-start.5
  0.7 0.6 copy-done.8
  1.3 0.0 copy-done.4
  1.3 0.0 copy-done.6
  1.3 0.0 copy-done.7
  1.4 0.0 copy-done.5
  1.4 0.0 copy-start
  1.4 1.0 %copy-done = bf16[1024,256]{1,0:T(8,128)(2,1)S(1)} copy-done((bf16[1024,256]{1,0:T(8,128)(2,1)S(1)}, bf16[1024,256]{1,0:T(8,128)(2,1)}, u32[]{:S(2)}) %copy-start) | copy-done | bytes 524312
  2.4 0.0 copy-start.1
  2.4 0.9 %copy-done.1 = bf16[16,32,256]{2,1,0:T(8,128)(2,1)S(1)} copy-done((bf16[16,32,256]{2,1,0:T(8,128)(2,1)S(1)}, bf16[16,32,256]{2,1,0:T(8,128)(2,1)}, u32[]{:S(2)}) %copy-start.1) | copy-done | bytes 262168
  3.4 0.0 copy-start.2
  3.4 0.8 %copy-done.2 = bf16[1024,32]{0,1:T(8,128)(2,1)S(1)} copy-done((bf16[1024,32]{0,1:T(8,128)(2,1)S(1)}, bf16[1024,32]{0,1:T(8,128)(2,1)}, u32[]{:S(2)}) %copy-start.2) | copy-done | bytes 65560
  4.2 0.0 copy-start.3
  4.2 0.7 copy-done.3
  4.9 63.6 %river.1 = (f32[16,256]{1,0:T(8,128)S(1)}, f32[32,1024]{1,0:T(8,128)S(1)}, f32[1024,256]{1,0:T(8,128)S(1)}, f32[1,1024]{1,0:T(1,128)S(1)}, f32[1,256]{1,0:T(1,128)S(1)}) custom-call(bf16[16,32,256]{2,1,0:T(8,128)(2,1)S(1)} %copy-done.1, bf16[32,1024]{1,0:T(8,128)(2,1)S(1)} %bitcast.10, bf16[1024,256]{1,0:T(8,128)(2,1)S(1)} %copy-done, ...), custom_call_target="tpu_custom_call" | custom-call | tf_op jit(solution)/shard_map/river/pallas_call | solution.py:412
  68.5 0.6 copy.19
  69.1 0.7 copy.20
  69.8 1.0 %copy.21 = f32[1024,256]{1,0:T(8,128)} copy(f32[1024,256]{1,0:T(8,128)S(1)} %get-tuple-element.22) | data formatting | bytes 2097152
  70.7 0.6 copy.22
  71.3 0.6 copy.23
Async XLA Ops:
  0.6 0.7 copy-start.8
  0.6 0.7 copy-start.4
  0.7 0.7 copy-start.6
  0.7 0.7 copy-start.7
  0.7 0.7 copy-start.5
  1.4 1.0 %copy-start = (bf16[1024,256]{1,0:T(8,128)(2,1)S(1)}, bf16[1024,256]{1,0:T(8,128)(2,1)}, u32[]{:S(2)}) copy-start(bf16[1024,256]{1,0:T(8,128)(2,1)} %w_rec.1) | copy-start | bytes 1572868
  2.4 0.9 %copy-start.1 = (bf16[16,32,256]{2,1,0:T(8,128)(2,1)S(1)}, bf16[16,32,256]{2,1,0:T(8,128)(2,1)}, u32[]{:S(2)}) copy-start(bf16[16,32,256]{2,1,0:T(8,128)(2,1)} %forcing.1) | copy-start | bytes 786436
  3.4 0.8 %copy-start.2 = (bf16[1024,32]{0,1:T(8,128)(2,1)S(1)}, bf16[1024,32]{0,1:T(8,128)(2,1)}, u32[]{:S(2)}) copy-start(bf16[1024,32]{0,1:T(8,128)(2,1)} %param.11) | copy-start | bytes 196612
  4.2 0.7 copy-start.3

commit v2 on v1

--- a/solution.py
+++ b/solution.py
@@ -17,7 +17,10 @@
 XROWS = 304
 GROWS = 1040
 CHUNK = 32
-SEMS = 200
+SEMS = 280
+PARTS = 4
+PROWS = 512 // PARTS
+OWNED = PROWS // 16
 NT = (((1,), (1,)), ((), ()))
 
 
@@ -125,14 +128,26 @@
 
 
 def kernel(
-    forcing, w_in_t, w_rec, bias, w_out, uh_shape, uh_scale, dest, cot,
+    forcing_h, w_in_t_h, w_rec_h, bias_h, w_out_h, uh_shape_h, uh_scale_h, dest_h, cot_h,
     o_flow, o_in, o_rec, o_bias, o_out,
-    W, WT, wcol, x, gates, cells, gz, gh, gcn, rd, grd,
+    w_in_t, w_rec, bias, w_out, uh_shape, uh_scale, dest, cot, load_sem,
+    W, WT, wcol, x, fac, cells, gz, gh, gcn, rd, grd,
     accA, accB, pad, adj, par, parb, route, fS, fR,
     bufA, rsA, zA, bufB, zB, xyB, outB, send, recv,
 ):
     p = Place()
     cp = Copies(send, recv)
+
+    loads = [
+        pltpu.make_async_copy(src, dst, load_sem.at[i])
+        for i, (src, dst) in enumerate((
+            (uh_shape_h, uh_shape), (uh_scale_h, uh_scale), (dest_h, dest), (cot_h, cot),
+            (w_rec_h, w_rec), (w_in_t_h, w_in_t), (bias_h, bias), (w_out_h, w_out),
+            (forcing_h, x.at[0:DAYS, 256:288]),
+        ))
+    ]
+    for load in loads:
+        load.start()
 
     barrier = pltpu.get_barrier_semaphore()
     partners = [p.core()]
@@ -143,6 +158,8 @@
         pl.semaphore_signal(barrier, inc=1, device_id=device, device_id_type=MESH)
 
     pad[...] = jnp.zeros_like(pad)
+    for load in loads[0:4]:
+        load.wait()
     uh = hydro(uh_shape[...], uh_scale[...])
     dest_row = dest[...]
     linked = dest_row >= 0
@@ -153,6 +170,9 @@
         row8 == 0, uh_shape[...], jnp.where(row8 == 1, uh_scale[...], index.astype(f32))
     )
     adj[0] = correlate(uh, cot[...], pad)
+
+    for load in loads[4:]:
+        load.wait()
 
     for k in range(0, 1024, 128):
         half = 0.5 if k // 256 == 2 else 0.25
@@ -176,10 +196,9 @@
     x[0, 0:256] = jnp.zeros((HID, REACH), bf16)
     ones = jnp.where(row16 < 3, 1.0, 0.0).astype(bf16)
     for t in range(DAYS):
-        x[t, 256:288] = forcing[t]
         x[t, 288:304] = ones
     x[DAYS, 256:304] = jnp.zeros((48, REACH), bf16)
-    cells[0] = jnp.zeros((HID, REACH), f32)
+    cells[...] = jnp.zeros((HID, REACH), f32)
 
     def forward(t, _):
         pre = jnp.dot(W[...], x[t], preferred_element_type=f32)
@@ -190,23 +209,29 @@
             tf = jnp.tanh(pre[HID + c : HID + c + CHUNK])
             tg = jnp.tanh(pre[2 * HID + c : 2 * HID + c + CHUNK])
             to = jnp.tanh(pre[3 * HID + c : 3 * HID + c + CHUNK])
-            cell = 0.5 * ((tf + 1.0) * cells[t, s] + (ti + 1.0) * tg)
-            gates[0, t, s] = ti
-            gates[1, t, s] = tf
-            gates[2, t, s] = tg
-            gates[3, t, s] = to
-            cells[t + 1, s] = cell
-            x[t + 1, s] = ((to + 1.0) * jnp.tanh(cell)).astype(bf16)
+            i1 = 1.0 + ti
+            f1 = 1.0 + tf
+            o1 = 1.0 + to
+            before = cells[s]
+            cell = 0.5 * (f1 * before + i1 * tg)
+            tc = jnp.tanh(cell)
+            h2 = o1 * tc
+            fac[0, t, s] = i1 * ((1.0 - ti) * tg)
+            fac[1, t, s] = f1 * ((1.0 - tf) * before)
+            fac[2, t, s] = i1 * (1.0 - tg * tg)
+            fac[3, t, s] = h2 * (1.0 - to)
+            fac[4, t, s] = o1 * (1.0 - tc * tc)
+            fac[5, t, s] = 0.5 * f1
+            cells[s] = cell
+            x[t + 1, s] = h2.astype(bf16)
         return 0
 
-    lax.fori_loop(0, 6, forward, 0)
-
     pl.semaphore_wait(barrier, len(partners))
-    adj_in = [cp(adj.at[0], adj.at[d], p.along(-d)) for d in range(1, 7)]
-    par_in = [cp(par.at[0], par.at[d], p.along(-d)) for d in range(1, 5)]
+    par_in = [cp(par.at[0], par.at[d], p.along(-d)) for d in range(4, 0, -1)]
+    adj_in = [cp(adj.at[0], adj.at[d], p.along(-d)) for d in range(6, 0, -1)]
     parb_in = [cp(par.at[0], parb.at[d - 1], p.along(d)) for d in (1, 2)]
 
-    lax.fori_loop(6, DAYS, forward, 0)
+    lax.fori_loop(0, DAYS, forward, 0)
     last = jnp.dot(W[1024:1040], x[DAYS], preferred_element_type=f32)
     rd[DAYS : DAYS + 1] = jnp.sum(last, axis=0, keepdims=True)
     readout = rd[1 : DAYS + 1]
@@ -251,30 +276,23 @@
             total = total + moved[0:16] + moved[16:32] + moved[32:48]
         return total
 
-    accA[...] = jnp.zeros_like(accA)
     accB[...] = jnp.zeros_like(accB)
-    gh[...] = jnp.zeros_like(gh)
-    gcn[...] = jnp.zeros_like(gcn)
 
     def elementwise(t):
-        gr = grd[pl.ds(t + 8, 1)]
+        gr = grd[t + 8 : t + 9]
         for c in range(0, HID, CHUNK):
             s = pl.ds(c, CHUNK)
-            w = jnp.concatenate([wcol[s], wcol[s]], 1)
-            ti = gates[0, t, s]
-            tf = gates[1, t, s]
-            tg = gates[2, t, s]
-            to = gates[3, t, s]
-            tc = jnp.tanh(cells[t + 1, s])
-            ghw = (w * gr + gh[s]) * (1.0 + to)
-            gc = ghw * (1.0 - tc * tc) + gcn[s]
-            gci = gc * (1.0 + ti)
-            gcf = gc * (1.0 + tf)
-            gz[c : c + CHUNK] = (gci * ((1.0 - ti) * tg)).astype(bf16)
-            gz[HID + c : HID + c + CHUNK] = (gcf * ((1.0 - tf) * cells[t, s])).astype(bf16)
-            gz[2 * HID + c : 2 * HID + c + CHUNK] = (gci * (1.0 - tg * tg)).astype(bf16)
-            gz[3 * HID + c : 3 * HID + c + CHUNK] = (ghw * ((1.0 - to) * tc)).astype(bf16)
-            gcn[s] = gcf * 0.5
+            ghc = jnp.concatenate([wcol[s], wcol[s]], 1) * gr
+            if t < DAYS - 1:
+                ghc = ghc + gh[s]
+            gc = ghc * fac[4, t, s]
+            if t < DAYS - 1:
+                gc = gc + gcn[s]
+            gz[c : c + CHUNK] = (gc * fac[0, t, s]).astype(bf16)
+            gz[HID + c : HID + c + CHUNK] = (gc * fac[1, t, s]).astype(bf16)
+            gz[2 * HID + c : 2 * HID + c + CHUNK] = (gc * fac[2, t, s]).astype(bf16)
+            gz[3 * HID + c : 3 * HID + c + CHUNK] = (ghc * fac[3, t, s]).astype(bf16)
+            gcn[s] = gc * fac[5, t, s]
 
     def read_rows(row):
         hi, mid, _ = split3(row)
@@ -288,30 +306,43 @@
             accB[0, j] += small[0:24, j * 128 : (j + 1) * 128]
             accB[1, j] += small[24:48, j * 128 : (j + 1) * 128]
 
-    def backward(i, _):
-        t = DAYS - 1 - i
-        elementwise(t)
+    def carry(t):
         gh[...] = jnp.dot(WT[...], gz[0:1024], preferred_element_type=f32)
-        gz[1024:1040] = read_rows(grd[pl.ds(t + 7, 1)])
-        accA[...] += lax.dot_general(gz[...], x[t, 0:256], NT, preferred_element_type=f32)
-        inputs_grad(t)
-        return 0
-
-    lax.fori_loop(0, 5, backward, 0)
-    for n in (0, 1):
-        for copy in flow_in:
-            copy.wait_recv()
-        fS[n + 1] = convolve(uh, runoff + inflow(n), pad)
-        flow_in = send_flow(n + 1)
-        lax.fori_loop(5 + 5 * n, 10 + 5 * n, backward, 0)
+
+    def rec_grad(t, s):
+        term = lax.dot_general(gz[s], x[t, 0:256], NT, preferred_element_type=f32)
+        accA[s] = term if t == DAYS - 1 else accA[s] + term
 
     own = p.r * 512
     other = (1 - p.r) * 512
     core = p.core()
-    core_in = [
-        cp(accA.at[rows(other + c * 256, 256)], bufA.at[pl.ds(c * 256, 256)], core)
-        for c in range(2)
-    ]
+    for t in range(DAYS - 1, 0, -1):
+        elementwise(t)
+        gz[1024:1040] = read_rows(grd[t + 7 : t + 8])
+        if t > 1:
+            carry(t)
+            rec_grad(t, slice(0, GROWS))
+        else:
+            rec_grad(t, rows(other, 512))
+            core_in = [
+                cp(
+                    accA.at[rows(other + c * PROWS, PROWS)],
+                    bufA.at[pl.ds(c * PROWS, PROWS)],
+                    core,
+                )
+                for c in range(PARTS)
+            ]
+            carry(t)
+            rec_grad(t, rows(own, 512))
+            rec_grad(t, slice(1024, GROWS))
+        inputs_grad(t)
+        if t in (11, 6):
+            n = 0 if t == 11 else 1
+            for copy in flow_in:
+                copy.wait_recv()
+            fS[n + 1] = convolve(uh, runoff + inflow(n), pad)
+            flow_in = send_flow(n + 1)
+
     elementwise(0)
     inputs_grad(0)
     last = lax.dot_general(
@@ -323,14 +354,15 @@
     core_b = cp(accB.at[1 - p.r], bufB, core)
 
     plane_in = []
-    for c in range(2):
+    for c in range(PARTS):
         core_in[c].wait_recv()
-        for k in range(0, 256, 64):
-            accA[rows(own + c * 256 + k, 64)] += bufA[c * 256 + k : c * 256 + k + 64]
+        for k in range(0, PROWS, 64):
+            accA[rows(own + c * PROWS + k, 64)] += bufA[c * PROWS + k : c * PROWS + k + 64]
         batch = []
         for d in range(1, 16):
             device, q = p.plane(d)
-            batch.append(cp(accA.at[rows(own + c * 256 + q * 16, 16)], rsA.at[c, d - 1], device))
+            part = accA.at[rows(own + c * PROWS + q * OWNED, OWNED)]
+            batch.append(cp(part, rsA.at[c, d - 1], device))
         plane_in.append(batch)
     core_b.wait_recv()
     accB[p.r] += bufB[...]
@@ -344,8 +376,8 @@
     o_flow[...] = convolve(uh, runoff + inflow(2), pad)
 
     line_in = []
-    for c in range(2):
-        total = accA[rows(own + c * 256 + p.q * 16, 16)]
+    for c in range(PARTS):
+        total = accA[rows(own + c * PROWS + p.q * OWNED, OWNED)]
         for d in range(1, 16):
             plane_in[c][d - 1].wait_recv()
             total = total + rsA[c, d - 1]
@@ -363,13 +395,13 @@
     factor = jnp.where(p.r == 0, 0.0625, 0.125).astype(f32)
     gathered = []
     passed = []
-    for c in range(2):
+    for c in range(PARTS):
         for copy in line_in[c]:
             copy.wait_recv()
         total = zA[c, 0]
         for z in range(1, 8):
             total = total + zA[c, z]
-        mine = o_rec.at[rows(own + c * 256 + p.q * 16, 16)]
+        mine = o_rec.at[rows(own + c * PROWS + p.q * OWNED, OWNED)]
         mine[...] = total * factor
         gathered.append([cp(mine, mine, p.plane(d)[0]) for d in range(1, 16)])
         passed.append(cp(mine, mine, core))
@@ -382,10 +414,10 @@
     mine = outB.at[p.r, p.z]
     gathered_b = [cp(mine, mine, p.line(d)[0]) for d in range(1, 8)]
     passed.append(cp(mine, mine, core))
-    for c in range(2):
+    for c in range(PARTS):
         for d in range(1, 16):
             gathered[c][d - 1].wait_recv()
-            piece = o_rec.at[rows(own + c * 256 + p.plane_from(d) * 16, 16)]
+            piece = o_rec.at[rows(own + c * PROWS + p.plane_from(d) * OWNED, OWNED)]
             passed.append(cp(piece, piece, core))
     for d in range(1, 8):
         gathered_b[d - 1].wait_recv()
@@ -405,28 +437,48 @@
     cp.drain()
 
 
+def write_out(*refs):
+    copies = [
+        pltpu.make_async_copy(refs[i], refs[5 + i], refs[10].at[i]) for i in range(5)
+    ]
+    for copy in copies:
+        copy.start()
+    for copy in copies:
+        copy.wait()
+
+
 def per_device(
     forcing, w_in, w_rec, bias, w_out, uh_shape, uh_scale, reach_tier, reach_dest, out_cot
 ):
     vmem = pl.BlockSpec(memory_space=VMEM)
-    flow, g_in, g_rec, g_bias, g_out = pl.pallas_call(
+    results = [
+        jax.ShapeDtypeStruct((DAYS, REACH), f32),
+        jax.ShapeDtypeStruct((FEAT, 1024), f32),
+        jax.ShapeDtypeStruct((1024, HID), f32),
+        jax.ShapeDtypeStruct((1, 1024), f32),
+        jax.ShapeDtypeStruct((1, HID), f32),
+    ]
+    held = pl.pallas_call(
         kernel,
-        out_shape=[
-            jax.ShapeDtypeStruct((DAYS, REACH), f32),
-            jax.ShapeDtypeStruct((FEAT, 1024), f32),
-            jax.ShapeDtypeStruct((1024, HID), f32),
-            jax.ShapeDtypeStruct((1, 1024), f32),
-            jax.ShapeDtypeStruct((1, HID), f32),
-        ],
-        in_specs=[vmem] * 9,
+        out_shape=results,
+        in_specs=[pl.BlockSpec(memory_space=pltpu.HBM)] * 9,
         out_specs=[vmem] * 5,
         scratch_shapes=[
+            VMEM((FEAT, 1024), bf16),
+            VMEM((1024, HID), bf16),
+            VMEM((1, 1024), f32),
+            VMEM((1, HID), f32),
+            VMEM((1, REACH), f32),
+            VMEM((1, REACH), f32),
+            VMEM((1, REACH), jnp.int32),
+            VMEM((DAYS, REACH), f32),
+            pltpu.SemaphoreType.DMA((9,)),
             VMEM((GROWS, XROWS), bf16),
             VMEM((HID, 1024), bf16),
             VMEM((HID, 128), f32),
             VMEM((DAYS + 1, XROWS, REACH), bf16),
-            VMEM((4, DAYS, HID, REACH), f32),
-            VMEM((DAYS + 1, HID, REACH), f32),
+            VMEM((6, DAYS, HID, REACH), f32),
+            VMEM((HID, REACH), f32),
             VMEM((GROWS, REACH), bf16),
             VMEM((HID, REACH), f32),
             VMEM((HID, REACH), f32),
@@ -442,8 +494,8 @@
             VMEM((3, DAYS, REACH), f32),
             VMEM((3, 2, DAYS, REACH), f32),
             VMEM((512, HID), f32),
-            VMEM((2, 15, 16, HID), f32),
-            VMEM((2, 8, 16, HID), f32),
+            VMEM((PARTS, 15, OWNED, HID), f32),
+            VMEM((PARTS, 8, OWNED, HID), f32),
             VMEM((8, 24, 128), f32),
             VMEM((7, 24, 128), f32),
             VMEM((16, 24, 128), f32),
@@ -456,16 +508,29 @@
         ),
         name="river",
     )(
-        forcing,
-        w_in.T,
-        w_rec,
-        bias.reshape(1, 1024),
-        w_out.reshape(1, HID),
-        uh_shape.reshape(1, REACH),
-        uh_scale.reshape(1, REACH),
-        reach_dest.reshape(1, REACH),
-        out_cot,
+        *(
+            pltpu.with_memory_space_constraint(operand, pltpu.HBM)
+            for operand in (
+                forcing,
+                w_in.T,
+                w_rec,
+                bias.reshape(1, 1024),
+                w_out.reshape(1, HID),
+                uh_shape.reshape(1, REACH),
+                uh_scale.reshape(1, REACH),
+                reach_dest.reshape(1, REACH),
+                out_cot,
+            )
+        )
     )
+    flow, g_in, g_rec, g_bias, g_out = pl.pallas_call(
+        write_out,
+        out_shape=results,
+        in_specs=[vmem] * 5,
+        out_specs=[pl.BlockSpec(memory_space=pltpu.HBM)] * 5,
+        scratch_shapes=[pltpu.SemaphoreType.DMA((5,))],
+        name="write_out",
+    )(*held)
     return (flow, g_in.T, g_rec, g_bias.reshape(1024), g_out.reshape(HID))
 
 

time: 72.2 us -> 69.3 us (0.960)
  local copies, waits for them, and re-layouts: 7.64 us -> 3.34 us
  Pallas kernels: 63.6 us -> 65.2 us
    unnamed x23 -> x10, local copies, waits for them, and re-layouts: 7.64 us -> 3.34 us
    pallas_call x1 -> x2, Pallas kernels: 63.6 us -> 65.2 us  [the longest x1 62.8 us: per_device(): pl.pallas_call(kernel, out_shape=results, in_specs=[pl.BlockSpec(memory_s...]
where the time goes in v2:
time: 69.3 us; the launch traced here: 69.2 us
  Pallas kernels  65.2 us (94%)
  local copies, waits for them, and re-layouts  3.34 us (5%)
    pallas_call x1, Pallas kernels, per_device(): pl.pallas_call(kernel, out_shape=results, in_specs=[pl.BlockSpec(memory_s...  62.8 us
    unnamed x10, local copies, waits for them, and re-layouts  3.34 us
    pallas_call x1, Pallas kernels, per_device(): pl.pallas_call(write_out, out_shape=results, in_specs=[vmem] * 5, out_spe...  2.39 us

profile of v2, /device:TPU:1, one launch (start us, length us, event | category | flops | bytes accessed | tf_op | source)
XLA Modules:
  0.0 69.2 jit_solution(16745099513352084450)
XLA Ops:
  0.6 62.8 %river.1 = (f32[16,256]{1,0:T(8,128)S(1)}, f32[32,1024]{1,0:T(8,128)S(1)}, f32[1024,256]{1,0:T(8,128)S(1)}, f32[1,1024]{1,0:T(1,128)S(1)}, f32[1,256]{1,0:T(1,128)S(1)}) custom-call(bf16[16,32,256]{2,1,0:T(8,128)(2,1)} %forcing_h.1, bf16[32,1024]{1,0:T(8,128)(2,1)} %bitcast.9, bf16[1024,256]{1,0:T(8,128)(2,1)} %w_rec_h.1, f32[1,1024]{1,0:T(1,128)} %bitcast.10, ...), custom_call_target="tpu_custom_call" | custom-call | tf_op jit(solution)/shard_map/river/pallas_call | solution.py:461
  63.4 0.0 copy-start
  63.4 1.0 %copy-done = f32[1024,256]{1,0:T(8,128)} copy-done((f32[1024,256]{1,0:T(8,128)}, f32[1024,256]{1,0:T(8,128)S(1)}, u32[]{:S(2)}) %copy-start) | copy-done | bytes 1048600
  64.4 0.0 copy-start.1
  64.4 0.7 copy-done.1
  65.0 0.0 copy-start.2
  65.0 0.6 copy-done.2
  65.6 0.0 copy-start.3
  65.6 0.6 copy-done.3
  66.2 0.0 copy-start.4
  66.2 0.5 copy-done.4
  66.8 2.4 %write_out.1 = (f32[16,256]{1,0:T(8,128)}, f32[32,1024]{1,0:T(8,128)}, f32[1024,256]{1,0:T(8,128)}, f32[1,1024]{1,0:T(1,128)}, f32[1,256]{1,0:T(1,128)}) custom-call(f32[16,256]{1,0:T(8,128)} %copy-done.2, f32[32,1024]{1,0:T(8,128)} %copy-done.1, f32[1024,256]{1,0:T(8,128)} %copy-done, f32[1,1024]{1,0:T(1,128)} %copy-done.3, f32[1,256]{1,0:T(1,128)} %copy-done.4), custom_call_target="tpu_custom_call" | custom-call | tf_op jit(solution)/shard_map/write_out/pallas_call | solution.py:526
Async XLA Ops:
  63.4 1.0 %copy-start = (f32[1024,256]{1,0:T(8,128)}, f32[1024,256]{1,0:T(8,128)S(1)}, u32[]{:S(2)}) copy-start(f32[1024,256]{1,0:T(8,128)S(1)} %get-tuple-element.17.refs_2_) | copy-start | bytes 3145732
  64.4 0.7 copy-start.1
  65.0 0.6 copy-start.2
  65.6 0.6 copy-start.3
  66.2 0.5 copy-start.4

commit v3 on v2

--- a/solution.py
+++ b/solution.py
@@ -17,7 +17,7 @@
 XROWS = 304
 GROWS = 1040
 CHUNK = 32
-SEMS = 280
+SEMS = 64
 PARTS = 4
 PROWS = 512 // PARTS
 OWNED = PROWS // 16
@@ -61,9 +61,8 @@
         self.recv = recv
         self.all = []
 
-    def __call__(self, src, dst, device):
-        i = len(self.all)
-        copy = pltpu.make_async_remote_copy(
+    def describe(self, i, src, dst, device):
+        return pltpu.make_async_remote_copy(
             src_ref=src,
             dst_ref=dst,
             send_sem=self.send.at[i],
@@ -71,13 +70,24 @@
             device_id=device,
             device_id_type=MESH,
         )
-        copy.start()
-        self.all.append(copy)
-        return copy
+
+    def __call__(self, src, dst, device):
+        return self.many([(src, dst, device)], src)
+
+    def many(self, copies, whole):
+        i = len(self.all)
+        for src, dst, device in copies:
+            self.describe(i, src, dst, device).start()
+        self.all.append(self.describe(i, whole, whole, copies[0][2]))
+        return self.all[-1]
 
     def drain(self):
         for copy in self.all:
             copy.wait_send()
+
+
+PLANE = sorted(range(1, 16), key=lambda d: (-min(d // 4, 4 - d // 4) - min(d % 4, 4 - d % 4), d))
+LINE = (4, 3, 5, 2, 6, 1, 7)
 
 
 def rows(start, size):
@@ -132,11 +142,19 @@
     o_flow, o_in, o_rec, o_bias, o_out,
     w_in_t, w_rec, bias, w_out, uh_shape, uh_scale, dest, cot, load_sem,
     W, WT, wcol, x, fac, cells, gz, gh, gcn, rd, grd,
-    accA, accB, pad, adj, par, parb, route, fS, fR,
+    accA, accB, pad, adj, route, fS, fR,
     bufA, rsA, zA, bufB, zB, xyB, outB, send, recv,
 ):
     p = Place()
     cp = Copies(send, recv)
+
+    barrier = pltpu.get_barrier_semaphore()
+    partners = [p.along(d) for d in (6, 5, 4, 3, 2, 1, -6, -5, -4, -3, -2, -1)]
+    partners += [p.plane(d)[0] for d in PLANE]
+    partners += [p.line(d)[0] for d in LINE]
+    partners += [p.core()]
+    for device in partners:
+        pl.semaphore_signal(barrier, inc=1, device_id=device, device_id_type=MESH)
 
     loads = [
         pltpu.make_async_copy(src, dst, load_sem.at[i])
@@ -149,14 +167,6 @@
     for load in loads:
         load.start()
 
-    barrier = pltpu.get_barrier_semaphore()
-    partners = [p.core()]
-    partners += [p.plane(d)[0] for d in range(1, 16)]
-    partners += [p.line(d)[0] for d in range(1, 8)]
-    partners += [p.along(d) for d in (1, 2, 3, 4, 5, 6, -1, -2, -3, -4, -5, -6)]
-    for device in partners:
-        pl.semaphore_signal(barrier, inc=1, device_id=device, device_id_type=MESH)
-
     pad[...] = jnp.zeros_like(pad)
     for load in loads[0:4]:
         load.wait()
@@ -165,11 +175,12 @@
     linked = dest_row >= 0
     ahead = jnp.right_shift(dest_row, 9) - p.b
     index = jnp.where(linked, ahead * REACH + jnp.bitwise_and(dest_row, REACH - 1), -1)
+    adj[0, 0:16] = correlate(uh, cot[...], pad)
     row8 = lax.broadcasted_iota(jnp.int32, (8, REACH), 0)
-    par[0] = jnp.where(
+    adj[0, 16:24] = jnp.where(
         row8 == 0, uh_shape[...], jnp.where(row8 == 1, uh_scale[...], index.astype(f32))
     )
-    adj[0] = correlate(uh, cot[...], pad)
+    fS[0, 16:24] = jnp.broadcast_to(index.astype(f32), (8, REACH))
 
     for load in loads[4:]:
         load.wait()
@@ -227,28 +238,29 @@
         return 0
 
     pl.semaphore_wait(barrier, len(partners))
-    par_in = [cp(par.at[0], par.at[d], p.along(-d)) for d in range(4, 0, -1)]
-    adj_in = [cp(adj.at[0], adj.at[d], p.along(-d)) for d in range(6, 0, -1)]
-    parb_in = [cp(par.at[0], parb.at[d - 1], p.along(d)) for d in (1, 2)]
-
+    adj_in = [
+        cp(adj.at[0, 0 : 24 if d < 5 else 16], adj.at[d, 0 : 24 if d < 5 else 16], p.along(-d))
+        for d in range(6, 0, -1)
+    ]
     lax.fori_loop(0, DAYS, forward, 0)
     last = jnp.dot(W[1024:1040], x[DAYS], preferred_element_type=f32)
     rd[DAYS : DAYS + 1] = jnp.sum(last, axis=0, keepdims=True)
     readout = rd[1 : DAYS + 1]
 
     runoff = jnp.maximum(readout, 0.0) + jnp.log1p(jnp.exp(-jnp.abs(readout)))
-    fS[0] = convolve(uh, runoff, pad)
+    fS[0, 0:16] = convolve(uh, runoff, pad)
 
     def send_flow(n):
-        return [cp(fS.at[n], fR.at[n, d - 1], p.along(d)) for d in (1, 2)]
+        size = 24 if n == 0 else 16
+        return [cp(fS.at[n, 0:size], fR.at[n, d - 1, 0:size], p.along(d)) for d in (2, 1)]
 
     flow_in = send_flow(0)
 
-    for copy in par_in + adj_in:
+    for copy in adj_in:
         copy.wait_recv()
-    level = [adj[d] for d in range(7)]
-    kernels = [uh] + [hydro(par[d, 0:1], par[d, 1:2]) for d in range(1, 5)]
-    indices = [index] + [par[d, 2:3].astype(jnp.int32) for d in range(1, 5)]
+    level = [adj[d, 0:16] for d in range(7)]
+    kernels = [uh] + [hydro(adj[d, 16:17], adj[d, 17:18]) for d in range(1, 5)]
+    indices = [index] + [adj[d, 18:19].astype(jnp.int32) for d in range(1, 5)]
     start = level
     for count in (5, 3, 1):
         level = [
@@ -260,17 +272,10 @@
     grd[0:8] = jnp.zeros((8, REACH), f32)
     grd[8:24] = grad_read
 
-    for copy in parb_in:
-        copy.wait_recv()
-    target = lax.broadcasted_iota(jnp.int32, (REACH, REACH), 0)
-    for j in range(3):
-        source = index if j == 0 else parb[j - 1, 2:3].astype(jnp.int32)
-        route[j] = jnp.where(target == source - j * REACH, 1.0, 0.0).astype(bf16)
-
     def inflow(n):
         total = jnp.zeros((DAYS, REACH), f32)
         for j in range(3):
-            flow = fS[n] if j == 0 else fR[n, j - 1]
+            flow = fS[n, 0:16] if j == 0 else fR[n, j - 1, 0:16]
             parts = jnp.concatenate(split3(flow), 0).astype(bf16)
             moved = lax.dot_general(parts, route[j], NT, preferred_element_type=f32)
             total = total + moved[0:16] + moved[16:32] + moved[32:48]
@@ -336,12 +341,15 @@
             rec_grad(t, rows(own, 512))
             rec_grad(t, slice(1024, GROWS))
         inputs_grad(t)
-        if t in (11, 6):
-            n = 0 if t == 11 else 1
+        if t == 8:
             for copy in flow_in:
                 copy.wait_recv()
-            fS[n + 1] = convolve(uh, runoff + inflow(n), pad)
-            flow_in = send_flow(n + 1)
+            target = lax.broadcasted_iota(jnp.int32, (REACH, REACH), 0)
+            for j in range(3):
+                source = index if j == 0 else fR[0, j - 1, 16:17].astype(jnp.int32)
+                route[j] = jnp.where(target == source - j * REACH, 1.0, 0.0).astype(bf16)
+            fS[1, 0:16] = convolve(uh, runoff + inflow(0), pad)
+            flow_in = send_flow(1)
 
     elementwise(0)
     inputs_grad(0)
@@ -359,70 +367,74 @@
         for k in range(0, PROWS, 64):
             accA[rows(own + c * PROWS + k, 64)] += bufA[c * PROWS + k : c * PROWS + k + 64]
         batch = []
-        for d in range(1, 16):
+        for d in PLANE:
             device, q = p.plane(d)
             part = accA.at[rows(own + c * PROWS + q * OWNED, OWNED)]
-            batch.append(cp(part, rsA.at[c, d - 1], device))
-        plane_in.append(batch)
+            batch.append((part, rsA.at[c, d - 1], device))
+        plane_in.append(cp.many(batch, rsA.at[c]))
     core_b.wait_recv()
     accB[p.r] += bufB[...]
-    line_b = []
+    batch = []
+    for d in LINE:
+        device, z = p.line(d)
+        batch.append((accB.at[p.r, z], zB.at[d - 1], device))
+    line_b = cp.many(batch, zB)
+
+    for copy in flow_in:
+        copy.wait_recv()
+    fS[2, 0:16] = convolve(uh, runoff + inflow(1), pad)
+    flow_in = send_flow(2)
+
+    line_in = []
+    for c in range(PARTS):
+        plane_in[c].wait_recv()
+        total = accA[rows(own + c * PROWS + p.q * OWNED, OWNED)]
+        for d in range(1, 16):
+            total = total + rsA[c, d - 1]
+        zA[c, p.z] = total
+        mine = zA.at[c, p.z]
+        line_in.append(
+            cp.many([(mine, mine, p.line(d)[0]) for d in LINE], rsA.at[c, 0:7])
+        )
+    line_b.wait_recv()
+    total = accB[p.r, p.z]
     for d in range(1, 8):
-        device, z = p.line(d)
-        line_b.append(cp(accB.at[p.r, z], zB.at[d - 1], device))
+        total = total + zB[d - 1]
+    xyB[p.q] = total
+    mine = xyB.at[p.q]
+    plane_b = cp.many([(mine, mine, p.plane(d)[0]) for d in PLANE], xyB.at[0:15])
 
     for copy in flow_in:
         copy.wait_recv()
     o_flow[...] = convolve(uh, runoff + inflow(2), pad)
-
-    line_in = []
-    for c in range(PARTS):
-        total = accA[rows(own + c * PROWS + p.q * OWNED, OWNED)]
-        for d in range(1, 16):
-            plane_in[c][d - 1].wait_recv()
-            total = total + rsA[c, d - 1]
-        zA[c, p.z] = total
-        mine = zA.at[c, p.z]
-        line_in.append([cp(mine, mine, p.line(d)[0]) for d in range(1, 8)])
-    total = accB[p.r, p.z]
-    for d in range(1, 8):
-        line_b[d - 1].wait_recv()
-        total = total + zB[d - 1]
-    xyB[p.q] = total
-    mine = xyB.at[p.q]
-    plane_b = [cp(mine, mine, p.plane(d)[0]) for d in range(1, 16)]
 
     factor = jnp.where(p.r == 0, 0.0625, 0.125).astype(f32)
     gathered = []
     passed = []
     for c in range(PARTS):
-        for copy in line_in[c]:
-            copy.wait_recv()
+        line_in[c].wait_recv()
         total = zA[c, 0]
         for z in range(1, 8):
             total = total + zA[c, z]
         mine = o_rec.at[rows(own + c * PROWS + p.q * OWNED, OWNED)]
         mine[...] = total * factor
-        gathered.append([cp(mine, mine, p.plane(d)[0]) for d in range(1, 16)])
-        passed.append(cp(mine, mine, core))
-    for copy in plane_b:
-        copy.wait_recv()
+        gathered.append(
+            cp.many([(mine, mine, p.plane(d)[0]) for d in PLANE], rsA.at[c])
+        )
+    plane_b.wait_recv()
     total = xyB[0]
     for q in range(1, 16):
         total = total + xyB[q]
     outB[p.r, p.z] = total
     mine = outB.at[p.r, p.z]
-    gathered_b = [cp(mine, mine, p.line(d)[0]) for d in range(1, 8)]
-    passed.append(cp(mine, mine, core))
+    gathered_b = cp.many([(mine, mine, p.line(d)[0]) for d in LINE], zB)
     for c in range(PARTS):
-        for d in range(1, 16):
-            gathered[c][d - 1].wait_recv()
-            piece = o_rec.at[rows(own + c * PROWS + p.plane_from(d) * OWNED, OWNED)]
-            passed.append(cp(piece, piece, core))
-    for d in range(1, 8):
-        gathered_b[d - 1].wait_recv()
-        piece = outB.at[p.r, p.line_from(d)]
-        passed.append(cp(piece, piece, core))
+        gathered[c].wait_recv()
+        whole = o_rec.at[rows(own + c * PROWS, PROWS)]
+        passed.append(cp(whole, whole, core))
+    gathered_b.wait_recv()
+    whole = outB.at[p.r]
+    passed.append(cp(whole, whole, core))
     for copy in passed:
         copy.wait_recv()
 
@@ -487,12 +499,10 @@
             VMEM((GROWS, HID), f32),
             VMEM((2, 8, 24, 128), f32),
             VMEM((32, REACH), f32),
-            VMEM((7, DAYS, REACH), f32),
-            VMEM((5, 8, REACH), f32),
-            VMEM((2, 8, REACH), f32),
+            VMEM((7, 24, REACH), f32),
             VMEM((3, REACH, REACH), bf16),
-            VMEM((3, DAYS, REACH), f32),
-            VMEM((3, 2, DAYS, REACH), f32),
+            VMEM((3, 24, REACH), f32),
+            VMEM((3, 2, 24, REACH), f32),
             VMEM((512, HID), f32),
             VMEM((PARTS, 15, OWNED, HID), f32),
             VMEM((PARTS, 8, OWNED, HID), f32),
@@ -526,8 +536,9 @@
     flow, g_in, g_rec, g_bias, g_out = pl.pallas_call(
         write_out,
         out_shape=results,
-        in_specs=[vmem] * 5,
+        in_specs=[pl.BlockSpec(memory_space=pl.ANY)] * 5,
         out_specs=[pl.BlockSpec(memory_space=pltpu.HBM)] * 5,
+        compiler_params=pltpu.CompilerParams(vmem_limit_bytes=2 * 2**20),
         scratch_shapes=[pltpu.SemaphoreType.DMA((5,))],
         name="write_out",
     )(*held)

time: 69.3 us -> 55.7 us (0.80)
  Pallas kernels: 65.2 us -> 54.9 us
  local copies, waits for them, and re-layouts: 3.34 us -> 0 us
    pallas_call x1, Pallas kernels: 62.8 us -> 53.9 us  [per_device(): pl.pallas_call(kernel, out_shape=results, in_specs=[pl.BlockSpec(memory_s...]
    unnamed x10 -> x0, local copies, waits for them, and re-layouts: 3.34 us -> none
    pallas_call x1, Pallas kernels: 2.39 us -> 1.07 us  [per_device(): pl.pallas_call(write_out, out_shape=results, in_specs=[pl.BlockSpec(memor...]
where the time goes in v3:
time: 55.7 us; the launch traced here: 55.6 us
  Pallas kernels  54.9 us (99%)
  between operations  0.64 us (1%)
    pallas_call x1, Pallas kernels, per_device(): pl.pallas_call(kernel, out_shape=results, in_specs=[pl.BlockSpec(memory_s...  53.9 us

profile of v3, /device:TPU:1, one launch (start us, length us, event | category | flops | bytes accessed | tf_op | source)
XLA Modules:
  0.0 55.6 jit_solution(8304824123692139970)
XLA Ops:
  0.6 53.9 %river.1 = (f32[16,256]{1,0:T(8,128)S(1)}, f32[32,1024]{1,0:T(8,128)S(1)}, f32[1024,256]{1,0:T(8,128)S(1)}, f32[1,1024]{1,0:T(1,128)S(1)}, f32[1,256]{1,0:T(1,128)S(1)}) custom-call(bf16[16,32,256]{2,1,0:T(8,128)(2,1)} %forcing_h.1, bf16[32,1024]{1,0:T(8,128)(2,1)} %bitcast.9, bf16[1024,256]{1,0:T(8,128)(2,1)} %w_rec_h.1, f32[1,1024]{1,0:T(1,128)} %bitcast.10, ...), custom_call_target="tpu_custom_call" | custom-call | tf_op jit(solution)/shard_map/river/pallas_call | solution.py:473
  54.5 1.1 %write_out.1 = (f32[16,256]{1,0:T(8,128)}, f32[32,1024]{1,0:T(8,128)}, f32[1024,256]{1,0:T(8,128)}, f32[1,1024]{1,0:T(1,128)}, f32[1,256]{1,0:T(1,128)}) custom-call(f32[16,256]{1,0:T(8,128)S(1)} %get-tuple-element.15.refs_0_, f32[32,1024]{1,0:T(8,128)S(1)} %get-tuple-element.16.refs_1_, f32[1024,256]{1,0:T(8,128)S(1)} %get-tuple-element.17.refs_2_, ...), custom_call_target="tpu_custom_call" | custom-call | tf_op jit(solution)/shard_map/write_out/pallas_call | solution.py:536

commit v4 on v3

--- a/solution.py
+++ b/solution.py
@@ -125,10 +125,10 @@
 def gather(blocks, index):
     halves = []
     for h in range(2):
-        idx = jnp.broadcast_to(index[:, h * 128 : (h + 1) * 128], (DAYS, 128))
+        idx = jnp.broadcast_to(index[:, h * 128 : (h + 1) * 128], (8, 128))
         lane = jnp.bitwise_and(idx, 127)
         block = jnp.right_shift(idx, 7)
-        total = jnp.zeros((DAYS, 128), f32)
+        total = jnp.zeros((8, 128), f32)
         for i in range(6):
             source = blocks[i // 2][:, (i % 2) * 128 : (i % 2 + 1) * 128]
             picked = jnp.take_along_axis(source, lane, axis=1)
@@ -142,7 +142,7 @@
     o_flow, o_in, o_rec, o_bias, o_out,
     w_in_t, w_rec, bias, w_out, uh_shape, uh_scale, dest, cot, load_sem,
     W, WT, wcol, x, fac, cells, gz, gh, gcn, rd, grd,
-    accA, accB, pad, adj, route, fS, fR,
+    accA, accB, pad, adj_late, adj_early, route, fS, fR,
     bufA, rsA, zA, bufB, zB, xyB, outB, send, recv,
 ):
     p = Place()
@@ -175,9 +175,11 @@
     linked = dest_row >= 0
     ahead = jnp.right_shift(dest_row, 9) - p.b
     index = jnp.where(linked, ahead * REACH + jnp.bitwise_and(dest_row, REACH - 1), -1)
-    adj[0, 0:16] = correlate(uh, cot[...], pad)
+    back = correlate(uh, cot[...], pad.at[0])
+    adj_early[0] = back[0:8]
+    adj_late[0, 0:8] = back[8:16]
     row8 = lax.broadcasted_iota(jnp.int32, (8, REACH), 0)
-    adj[0, 16:24] = jnp.where(
+    adj_late[0, 8:16] = jnp.where(
         row8 == 0, uh_shape[...], jnp.where(row8 == 1, uh_scale[...], index.astype(f32))
     )
     fS[0, 16:24] = jnp.broadcast_to(index.astype(f32), (8, REACH))
@@ -237,18 +239,24 @@
             x[t + 1, s] = h2.astype(bf16)
         return 0
 
+    lax.fori_loop(0, 5, forward, 0)
+
     pl.semaphore_wait(barrier, len(partners))
-    adj_in = [
-        cp(adj.at[0, 0 : 24 if d < 5 else 16], adj.at[d, 0 : 24 if d < 5 else 16], p.along(-d))
-        for d in range(6, 0, -1)
-    ]
-    lax.fori_loop(0, DAYS, forward, 0)
+    late_in = []
+    for d in range(6, 0, -1):
+        size = 16 if d < 5 else 8
+        late_in.append(
+            cp(adj_late.at[0, 0:size], adj_late.at[d, 0:size], p.along(-d))
+        )
+    early_in = [cp(adj_early.at[0], adj_early.at[d], p.along(-d)) for d in range(6, 0, -1)]
+
+    lax.fori_loop(5, DAYS, forward, 0)
     last = jnp.dot(W[1024:1040], x[DAYS], preferred_element_type=f32)
     rd[DAYS : DAYS + 1] = jnp.sum(last, axis=0, keepdims=True)
     readout = rd[1 : DAYS + 1]
 
     runoff = jnp.maximum(readout, 0.0) + jnp.log1p(jnp.exp(-jnp.abs(readout)))
-    fS[0, 0:16] = convolve(uh, runoff, pad)
+    fS[0, 0:16] = convolve(uh, runoff, pad.at[1])
 
     def send_flow(n):
         size = 24 if n == 0 else 16
@@ -256,21 +264,34 @@
 
     flow_in = send_flow(0)
 
-    for copy in adj_in:
-        copy.wait_recv()
-    level = [adj[d, 0:16] for d in range(7)]
-    kernels = [uh] + [hydro(adj[d, 16:17], adj[d, 17:18]) for d in range(1, 5)]
-    indices = [index] + [adj[d, 18:19].astype(jnp.int32) for d in range(1, 5)]
-    start = level
-    for count in (5, 3, 1):
-        level = [
-            start[j] + correlate(kernels[j], gather(level[j : j + 3], indices[j]), pad)
-            for j in range(count)
-        ]
-    grad_runoff = level[0]
-    grad_read = (0.5 * jnp.tanh(0.5 * readout) + 0.5) * grad_runoff
+    kernels, indices = {0: uh}, {0: index}
+    rate = 0.5 * jnp.tanh(0.5 * readout) + 0.5
+
+    def adjoint(copies, buffer, first):
+        start = {0: buffer[0, 0:8]}
+        for d in range(6, 0, -1):
+            copies[6 - d].wait_recv()
+            start[d] = buffer[d, 0:8]
+            if d < 5 and d not in kernels:
+                kernels[d] = hydro(buffer[d, 8:9], buffer[d, 9:10])
+                indices[d] = buffer[d, 10:11].astype(jnp.int32)
+        level = start
+        used = 4
+        for count in (5, 3, 1):
+            following = {}
+            for j in range(count - 1, -1, -1):
+                arrived = gather([level[j], level[j + 1], level[j + 2]], indices[j])
+                pad[used, first : first + 8] = arrived
+                total = start[j] + kernels[j][0:1] * arrived
+                for m in range(1, UHLEN):
+                    total = total + kernels[j][m : m + 1] * pad[used, first + m : first + m + 8]
+                following[j] = total
+                used += 1
+            level = following
+        return level[0]
+
+    grd[16:24] = rate[8:16] * adjoint(late_in, adj_late, 16)
     grd[0:8] = jnp.zeros((8, REACH), f32)
-    grd[8:24] = grad_read
 
     def inflow(n):
         total = jnp.zeros((DAYS, REACH), f32)
@@ -281,7 +302,6 @@
             total = total + moved[0:16] + moved[16:32] + moved[32:48]
         return total
 
-    accB[...] = jnp.zeros_like(accB)
 
     def elementwise(t):
         gr = grd[t + 8 : t + 9]
@@ -293,74 +313,56 @@
             gc = ghc * fac[4, t, s]
             if t < DAYS - 1:
                 gc = gc + gcn[s]
-            gz[c : c + CHUNK] = (gc * fac[0, t, s]).astype(bf16)
-            gz[HID + c : HID + c + CHUNK] = (gc * fac[1, t, s]).astype(bf16)
-            gz[2 * HID + c : 2 * HID + c + CHUNK] = (gc * fac[2, t, s]).astype(bf16)
-            gz[3 * HID + c : 3 * HID + c + CHUNK] = (ghc * fac[3, t, s]).astype(bf16)
+            gz[t, c : c + CHUNK] = (gc * fac[0, t, s]).astype(bf16)
+            gz[t, HID + c : HID + c + CHUNK] = (gc * fac[1, t, s]).astype(bf16)
+            gz[t, 2 * HID + c : 2 * HID + c + CHUNK] = (gc * fac[2, t, s]).astype(bf16)
+            gz[t, 3 * HID + c : 3 * HID + c + CHUNK] = (ghc * fac[3, t, s]).astype(bf16)
             gcn[s] = gc * fac[5, t, s]
 
     def read_rows(row):
         hi, mid, _ = split3(row)
         return jnp.where(row16 == 0, hi, jnp.where(row16 == 1, mid, 0.0)).astype(bf16)
 
-    def inputs_grad(t):
-        small = lax.dot_general(
-            x[t, 256:304], gz[0:1024], NT, preferred_element_type=f32
-        )
-        for j in range(8):
-            accB[0, j] += small[0:24, j * 128 : (j + 1) * 128]
-            accB[1, j] += small[24:48, j * 128 : (j + 1) * 128]
+    def inputs_grad():
+        for k in range(4):
+            total = jnp.zeros((48, 256), f32)
+            for t in range(DAYS - 1, -1, -1):
+                total = total + lax.dot_general(
+                    x[t, 256:304],
+                    gz[t, k * 256 : (k + 1) * 256],
+                    NT,
+                    preferred_element_type=f32,
+                )
+            for j in range(2):
+                part = total[:, j * 128 : (j + 1) * 128]
+                accB[0, 2 * k + j] = part[0:24]
+                accB[1, 2 * k + j] = part[24:48]
 
     def carry(t):
-        gh[...] = jnp.dot(WT[...], gz[0:1024], preferred_element_type=f32)
+        gh[...] = jnp.dot(WT[...], gz[t, 0:1024], preferred_element_type=f32)
 
     def rec_grad(t, s):
-        term = lax.dot_general(gz[s], x[t, 0:256], NT, preferred_element_type=f32)
+        term = lax.dot_general(gz[t, s], x[t, 0:256], NT, preferred_element_type=f32)
         accA[s] = term if t == DAYS - 1 else accA[s] + term
 
     own = p.r * 512
     other = (1 - p.r) * 512
     core = p.core()
-    for t in range(DAYS - 1, 0, -1):
+    for t in range(DAYS - 1, 1, -1):
         elementwise(t)
-        gz[1024:1040] = read_rows(grd[t + 7 : t + 8])
-        if t > 1:
-            carry(t)
-            rec_grad(t, slice(0, GROWS))
-        else:
-            rec_grad(t, rows(other, 512))
-            core_in = [
-                cp(
-                    accA.at[rows(other + c * PROWS, PROWS)],
-                    bufA.at[pl.ds(c * PROWS, PROWS)],
-                    core,
-                )
-                for c in range(PARTS)
-            ]
-            carry(t)
-            rec_grad(t, rows(own, 512))
-            rec_grad(t, slice(1024, GROWS))
-        inputs_grad(t)
-        if t == 8:
-            for copy in flow_in:
-                copy.wait_recv()
-            target = lax.broadcasted_iota(jnp.int32, (REACH, REACH), 0)
-            for j in range(3):
-                source = index if j == 0 else fR[0, j - 1, 16:17].astype(jnp.int32)
-                route[j] = jnp.where(target == source - j * REACH, 1.0, 0.0).astype(bf16)
-            fS[1, 0:16] = convolve(uh, runoff + inflow(0), pad)
-            flow_in = send_flow(1)
-
-    elementwise(0)
-    inputs_grad(0)
-    last = lax.dot_general(
-        read_rows(grd[DAYS + 7 : DAYS + 8]), x[DAYS, 0:256], NT, preferred_element_type=f32
-    )
-    out_row = jnp.sum(last + accA[1024:1040], axis=0, keepdims=True)
-    for j in range(2):
-        accB[1, j, 11:12] = out_row[:, j * 128 : (j + 1) * 128]
-    core_b = cp(accB.at[1 - p.r], bufB, core)
-
+        gz[t, 1024:1040] = read_rows(grd[t + 7 : t + 8])
+        carry(t)
+        rec_grad(t, slice(0, GROWS))
+        if t == 11:
+            grd[8:16] = rate[0:8] * adjoint(early_in, adj_early, 8)
+
+    elementwise(1)
+    rec_grad(1, rows(other, 512))
+    core_in = [
+        cp(accA.at[rows(other + c * PROWS, PROWS)], bufA.at[pl.ds(c * PROWS, PROWS)], core)
+        for c in range(PARTS)
+    ]
+    rec_grad(1, rows(own, 512))
     plane_in = []
     for c in range(PARTS):
         core_in[c].wait_recv()
@@ -372,6 +374,29 @@
             part = accA.at[rows(own + c * PROWS + q * OWNED, OWNED)]
             batch.append((part, rsA.at[c, d - 1], device))
         plane_in.append(cp.many(batch, rsA.at[c]))
+
+    gz[1, 1024:1040] = read_rows(grd[8:9])
+    rec_grad(1, slice(1024, GROWS))
+    carry(1)
+    elementwise(0)
+    inputs_grad()
+    last = lax.dot_general(
+        read_rows(grd[DAYS + 7 : DAYS + 8]), x[DAYS, 0:256], NT, preferred_element_type=f32
+    )
+    out_row = jnp.sum(last + accA[1024:1040], axis=0, keepdims=True)
+    for j in range(2):
+        accB[1, j, 11:12] = out_row[:, j * 128 : (j + 1) * 128]
+    core_b = cp(accB.at[1 - p.r], bufB, core)
+
+    for copy in flow_in:
+        copy.wait_recv()
+    target = lax.broadcasted_iota(jnp.int32, (REACH, REACH), 0)
+    for j in range(3):
+        source = index if j == 0 else fR[0, j - 1, 16:17].astype(jnp.int32)
+        route[j] = jnp.where(target == source - j * REACH, 1.0, 0.0).astype(bf16)
+    fS[1, 0:16] = convolve(uh, runoff + inflow(0), pad.at[2])
+    flow_in = send_flow(1)
+
     core_b.wait_recv()
     accB[p.r] += bufB[...]
     batch = []
@@ -379,11 +404,6 @@
         device, z = p.line(d)
         batch.append((accB.at[p.r, z], zB.at[d - 1], device))
     line_b = cp.many(batch, zB)
-
-    for copy in flow_in:
-        copy.wait_recv()
-    fS[2, 0:16] = convolve(uh, runoff + inflow(1), pad)
-    flow_in = send_flow(2)
 
     line_in = []
     for c in range(PARTS):
@@ -406,7 +426,8 @@
 
     for copy in flow_in:
         copy.wait_recv()
-    o_flow[...] = convolve(uh, runoff + inflow(2), pad)
+    fS[2, 0:16] = convolve(uh, runoff + inflow(1), pad.at[3])
+    flow_in = send_flow(2)
 
     factor = jnp.where(p.r == 0, 0.0625, 0.125).astype(f32)
     gathered = []
@@ -428,16 +449,22 @@
     outB[p.r, p.z] = total
     mine = outB.at[p.r, p.z]
     gathered_b = cp.many([(mine, mine, p.line(d)[0]) for d in LINE], zB)
-    for c in range(PARTS):
+
+    for copy in flow_in:
+        copy.wait_recv()
+    o_flow[...] = convolve(uh, runoff + inflow(2), pad.at[2])
+
+    for c in range(PARTS - 1):
         gathered[c].wait_recv()
         whole = o_rec.at[rows(own + c * PROWS, PROWS)]
         passed.append(cp(whole, whole, core))
     gathered_b.wait_recv()
     whole = outB.at[p.r]
+    passed_b = cp(whole, whole, core)
+    gathered[PARTS - 1].wait_recv()
+    whole = o_rec.at[rows(own + (PARTS - 1) * PROWS, PROWS)]
     passed.append(cp(whole, whole, core))
-    for copy in passed:
-        copy.wait_recv()
-
+    passed_b.wait_recv()
     for j in range(8):
         s = slice(j * 128, (j + 1) * 128)
         back = 0.25 if j >= 4 else 0.125
@@ -447,6 +474,8 @@
         if j < 2:
             o_out[:, s] = outB[1, j, 11:12] * 0.5
     cp.drain()
+    for copy in passed:
+        copy.wait_recv()
 
 
 def write_out(*refs):
@@ -491,15 +520,16 @@
             VMEM((DAYS + 1, XROWS, REACH), bf16),
             VMEM((6, DAYS, HID, REACH), f32),
             VMEM((HID, REACH), f32),
-            VMEM((GROWS, REACH), bf16),
+            VMEM((DAYS, GROWS, REACH), bf16),
             VMEM((HID, REACH), f32),
             VMEM((HID, REACH), f32),
             VMEM((24, REACH), f32),
             VMEM((24, REACH), f32),
             VMEM((GROWS, HID), f32),
             VMEM((2, 8, 24, 128), f32),
-            VMEM((32, REACH), f32),
-            VMEM((7, 24, REACH), f32),
+            VMEM((13, 32, REACH), f32),
+            VMEM((7, 16, REACH), f32),
+            VMEM((7, 8, REACH), f32),
             VMEM((3, REACH, REACH), bf16),
             VMEM((3, 24, REACH), f32),
             VMEM((3, 2, 24, REACH), f32),

time: 55.7 us -> 53.4 us (0.959)
  Pallas kernels: 54.9 us -> 52.7 us
    pallas_call x1, Pallas kernels: 53.9 us -> 51.6 us  [per_device(): pl.pallas_call(kernel, out_shape=results, in_specs=[pl.BlockSpec(memory_s...]
where the time goes in v4:
time: 53.4 us; the launch traced here: 53.3 us
  Pallas kernels  52.7 us (99%)
  between operations  0.64 us (1%)
    pallas_call x1, Pallas kernels, per_device(): pl.pallas_call(kernel, out_shape=results, in_specs=[pl.BlockSpec(memory_s...  51.6 us
    pallas_call x1, Pallas kernels, per_device(): pl.pallas_call(write_out, out_shape=results, in_specs=[pl.BlockSpec(memor...  1.07 us

profile of v4, /device:TPU:1, one launch (start us, length us, event | category | flops | bytes accessed | tf_op | source)
XLA Modules:
  0.0 53.3 jit_solution(17378477545702989162)
XLA Ops:
  0.6 51.6 %river.1 = (f32[16,256]{1,0:T(8,128)S(1)}, f32[32,1024]{1,0:T(8,128)S(1)}, f32[1024,256]{1,0:T(8,128)S(1)}, f32[1,1024]{1,0:T(1,128)S(1)}, f32[1,256]{1,0:T(1,128)S(1)}) custom-call(bf16[16,32,256]{2,1,0:T(8,128)(2,1)} %forcing_h.1, bf16[32,1024]{1,0:T(8,128)(2,1)} %bitcast.9, bf16[1024,256]{1,0:T(8,128)(2,1)} %w_rec_h.1, f32[1,1024]{1,0:T(1,128)} %bitcast.10, ...), custom_call_target="tpu_custom_call" | custom-call | tf_op jit(solution)/shard_map/river/pallas_call | solution.py:502
  52.2 1.1 %write_out.1 = (f32[16,256]{1,0:T(8,128)}, f32[32,1024]{1,0:T(8,128)}, f32[1024,256]{1,0:T(8,128)}, f32[1,1024]{1,0:T(1,128)}, f32[1,256]{1,0:T(1,128)}) custom-call(f32[16,256]{1,0:T(8,128)S(1)} %get-tuple-element.15.refs_0_, f32[32,1024]{1,0:T(8,128)S(1)} %get-tuple-element.16.refs_1_, f32[1024,256]{1,0:T(8,128)S(1)} %get-tuple-element.17.refs_2_, ...), custom_call_target="tpu_custom_call" | custom-call | tf_op jit(solution)/shard_map/write_out/pallas_call | solution.py:566

commit v5 on v4

--- a/solution.py
+++ b/solution.py
@@ -142,8 +142,8 @@
     o_flow, o_in, o_rec, o_bias, o_out,
     w_in_t, w_rec, bias, w_out, uh_shape, uh_scale, dest, cot, load_sem,
     W, WT, wcol, x, fac, cells, gz, gh, gcn, rd, grd,
-    accA, accB, pad, adj_late, adj_early, route, fS, fR,
-    bufA, rsA, zA, bufB, zB, xyB, outB, send, recv,
+    accA, accB, pad, adj_late, adj_early, turned, route, fS, fR,
+    bufA, rsA, zA, bufB, zB, xyB, outB, accT, bufT, zT, xyT, outT, send, recv,
 ):
     p = Place()
     cp = Copies(send, recv)
@@ -264,6 +264,9 @@
 
     flow_in = send_flow(0)
 
+    for t in range(1, DAYS):
+        turned[t - 1] = x[t, 0:256].T
+
     kernels, indices = {0: uh}, {0: index}
     rate = 0.5 * jnp.tanh(0.5 * readout) + 0.5
 
@@ -323,10 +326,10 @@
         hi, mid, _ = split3(row)
         return jnp.where(row16 == 0, hi, jnp.where(row16 == 1, mid, 0.0)).astype(bf16)
 
-    def inputs_grad():
+    def inputs_grad(days, first):
         for k in range(4):
             total = jnp.zeros((48, 256), f32)
-            for t in range(DAYS - 1, -1, -1):
+            for t in days:
                 total = total + lax.dot_general(
                     x[t, 256:304],
                     gz[t, k * 256 : (k + 1) * 256],
@@ -335,14 +338,17 @@
                 )
             for j in range(2):
                 part = total[:, j * 128 : (j + 1) * 128]
-                accB[0, 2 * k + j] = part[0:24]
-                accB[1, 2 * k + j] = part[24:48]
+                for i in range(2):
+                    term = part[16 * i : 16 * i + 16]
+                    accB[i, 2 * k + j] = term if first else accB[i, 2 * k + j] + term
+                row = slice(2 * k + j, 2 * k + j + 1)
+                accT[0, row] = part[32:33] if first else accT[0, row] + part[32:33]
 
     def carry(t):
         gh[...] = jnp.dot(WT[...], gz[t, 0:1024], preferred_element_type=f32)
 
     def rec_grad(t, s):
-        term = lax.dot_general(gz[t, s], x[t, 0:256], NT, preferred_element_type=f32)
+        term = jnp.dot(gz[t, s], turned[t - 1], preferred_element_type=f32)
         accA[s] = term if t == DAYS - 1 else accA[s] + term
 
     own = p.r * 512
@@ -363,6 +369,7 @@
         for c in range(PARTS)
     ]
     rec_grad(1, rows(own, 512))
+    inputs_grad(range(15, 9, -1), True)
     plane_in = []
     for c in range(PARTS):
         core_in[c].wait_recv()
@@ -379,14 +386,16 @@
     rec_grad(1, slice(1024, GROWS))
     carry(1)
     elementwise(0)
-    inputs_grad()
+    inputs_grad(range(9, -1, -1), False)
     last = lax.dot_general(
         read_rows(grd[DAYS + 7 : DAYS + 8]), x[DAYS, 0:256], NT, preferred_element_type=f32
     )
     out_row = jnp.sum(last + accA[1024:1040], axis=0, keepdims=True)
+    accT[1] = jnp.zeros((8, 128), f32)
     for j in range(2):
-        accB[1, j, 11:12] = out_row[:, j * 128 : (j + 1) * 128]
+        accT[1, j : j + 1] = out_row[:, j * 128 : (j + 1) * 128]
     core_b = cp(accB.at[1 - p.r], bufB, core)
+    core_t = cp(accT.at[1 - p.r], bufT, core)
 
     for copy in flow_in:
         copy.wait_recv()
@@ -404,6 +413,10 @@
         device, z = p.line(d)
         batch.append((accB.at[p.r, z], zB.at[d - 1], device))
     line_b = cp.many(batch, zB)
+    core_t.wait_recv()
+    zT[p.z] = accT[p.r] + bufT[...]
+    mine = zT.at[p.z]
+    line_t = cp.many([(mine, mine, p.line(d)[0]) for d in LINE], zT.at[0:7])
 
     line_in = []
     for c in range(PARTS):
@@ -423,6 +436,13 @@
     xyB[p.q] = total
     mine = xyB.at[p.q]
     plane_b = cp.many([(mine, mine, p.plane(d)[0]) for d in PLANE], xyB.at[0:15])
+    line_t.wait_recv()
+    total = zT[0]
+    for z in range(1, 8):
+        total = total + zT[z]
+    xyT[p.q] = total
+    mine = xyT.at[p.q]
+    plane_t = cp.many([(mine, mine, p.plane(d)[0]) for d in PLANE], xyT.at[0:15])
 
     for copy in flow_in:
         copy.wait_recv()
@@ -449,6 +469,13 @@
     outB[p.r, p.z] = total
     mine = outB.at[p.r, p.z]
     gathered_b = cp.many([(mine, mine, p.line(d)[0]) for d in LINE], zB)
+    plane_t.wait_recv()
+    total = xyT[0]
+    for q in range(1, 16):
+        total = total + xyT[q]
+    outT[p.r] = total
+    mine = outT.at[p.r]
+    passed_t = cp(mine, mine, core)
 
     for copy in flow_in:
         copy.wait_recv()
@@ -464,15 +491,16 @@
     gathered[PARTS - 1].wait_recv()
     whole = o_rec.at[rows(own + (PARTS - 1) * PROWS, PROWS)]
     passed.append(cp(whole, whole, core))
+    passed_t.wait_recv()
     passed_b.wait_recv()
     for j in range(8):
         s = slice(j * 128, (j + 1) * 128)
         back = 0.25 if j >= 4 else 0.125
-        o_in[0:24, s] = outB[0, j] * back
-        o_in[24:32, s] = outB[1, j, 0:8] * back
-        o_bias[:, s] = outB[1, j, 8:9] * back
+        o_in[0:16, s] = outB[0, j] * back
+        o_in[16:32, s] = outB[1, j] * back
+        o_bias[:, s] = outT[0, j : j + 1] * back
         if j < 2:
-            o_out[:, s] = outB[1, j, 11:12] * 0.5
+            o_out[:, s] = outT[1, j : j + 1] * 0.5
     cp.drain()
     for copy in passed:
         copy.wait_recv()
@@ -526,20 +554,26 @@
             VMEM((24, REACH), f32),
             VMEM((24, REACH), f32),
             VMEM((GROWS, HID), f32),
-            VMEM((2, 8, 24, 128), f32),
+            VMEM((2, 8, 16, 128), f32),
             VMEM((13, 32, REACH), f32),
             VMEM((7, 16, REACH), f32),
             VMEM((7, 8, REACH), f32),
+            VMEM((DAYS - 1, REACH, HID), bf16),
             VMEM((3, REACH, REACH), bf16),
             VMEM((3, 24, REACH), f32),
             VMEM((3, 2, 24, REACH), f32),
             VMEM((512, HID), f32),
             VMEM((PARTS, 15, OWNED, HID), f32),
             VMEM((PARTS, 8, OWNED, HID), f32),
-            VMEM((8, 24, 128), f32),
-            VMEM((7, 24, 128), f32),
-            VMEM((16, 24, 128), f32),
-            VMEM((2, 8, 24, 128), f32),
+            VMEM((8, 16, 128), f32),
+            VMEM((7, 16, 128), f32),
+            VMEM((16, 16, 128), f32),
+            VMEM((2, 8, 16, 128), f32),
+            VMEM((2, 8, 128), f32),
+            VMEM((8, 128), f32),
+            VMEM((8, 8, 128), f32),
+            VMEM((16, 8, 128), f32),
+            VMEM((2, 8, 128), f32),
             pltpu.SemaphoreType.DMA((SEMS,)),
             pltpu.SemaphoreType.DMA((SEMS,)),
         ],

time: 53.4 us -> 53.4 us (level)
  no operation moved by 1% of the time
where the time goes in v5:
time: 53.4 us; the launch traced here: 53.3 us
  Pallas kernels  52.6 us (99%)
  between operations  0.64 us (1%)
    pallas_call x1, Pallas kernels, per_device(): pl.pallas_call(kernel, out_shape=results, in_specs=[pl.BlockSpec(memory_s...  51.6 us
    pallas_call x1, Pallas kernels, per_device(): pl.pallas_call(write_out, out_shape=results, in_specs=[pl.BlockSpec(memor...  1.07 us

profile of v5, /device:TPU:1, one launch (start us, length us, event | category | flops | bytes accessed | tf_op | source)
XLA Modules:
  0.0 53.3 jit_solution(10710993748017511782)
XLA Ops:
  0.6 51.6 %river.1 = (f32[16,256]{1,0:T(8,128)S(1)}, f32[32,1024]{1,0:T(8,128)S(1)}, f32[1024,256]{1,0:T(8,128)S(1)}, f32[1,1024]{1,0:T(1,128)S(1)}, f32[1,256]{1,0:T(1,128)S(1)}) custom-call(bf16[16,32,256]{2,1,0:T(8,128)(2,1)} %forcing_h.1, bf16[32,1024]{1,0:T(8,128)(2,1)} %bitcast.9, bf16[1024,256]{1,0:T(8,128)(2,1)} %w_rec_h.1, f32[1,1024]{1,0:T(1,128)} %bitcast.10, ...), custom_call_target="tpu_custom_call" | custom-call | tf_op jit(solution)/shard_map/river/pallas_call | solution.py:530
  52.2 1.1 %write_out.1 = (f32[16,256]{1,0:T(8,128)}, f32[32,1024]{1,0:T(8,128)}, f32[1024,256]{1,0:T(8,128)}, f32[1,1024]{1,0:T(1,128)}, f32[1,256]{1,0:T(1,128)}) custom-call(f32[16,256]{1,0:T(8,128)S(1)} %get-tuple-element.15.refs_0_, f32[32,1024]{1,0:T(8,128)S(1)} %get-tuple-element.16.refs_1_, f32[1024,256]{1,0:T(8,128)S(1)} %get-tuple-element.17.refs_2_, ...), custom_call_target="tpu_custom_call" | custom-call | tf_op jit(solution)/shard_map/write_out/pallas_call | solution.py:600
